TPU v7x, 32 devices: a whole 2x2x4 slice. The times are simulated.
32 devices in a mesh: seq: 2 (over x), fsdp: 16 (over z, y, core).
Axes of the slice: x: 2, y: 2, z: 4, core: 2. Of those that a mesh axis runs over, the one named last changes fastest.
Arguments:
- inputs: bfloat16 [32, 1024, 768], P('fsdp', 'seq'), may hold values from -6 to 6
- out_grad: bfloat16 [32, 1024, 768], P('fsdp', 'seq'), may hold values from -6 to 6
- first_gain: bfloat16 [768], P(('seq', 'fsdp')), may hold values from 0.099609375 to 1.8984375
- first_shift: bfloat16 [768], P(('seq', 'fsdp')), may hold values from -3 to 3
- w_qkv: bfloat16 [768, 2304], P(('seq', 'fsdp')), may hold values from -0.21875 to 0.21875
- b_query: bfloat16 [768], P(('seq', 'fsdp')), may hold values from -3 to 3
- b_value: bfloat16 [768], P(('seq', 'fsdp')), may hold values from -3 to 3
- w_proj: bfloat16 [768, 768], P(('seq', 'fsdp')), may hold values from -0.875 to 0.875
- b_proj: bfloat16 [768], P(('seq', 'fsdp')), may hold values from -3 to 3
- second_gain: bfloat16 [768], P(('seq', 'fsdp')), may hold values from 0.099609375 to 1.8984375
- second_shift: bfloat16 [768], P(('seq', 'fsdp')), may hold values from -3 to 3
- w_up: bfloat16 [768, 3072], P(('seq', 'fsdp')), may hold values from -0.21875 to 0.21875
- b_up: bfloat16 [3072], P(('seq', 'fsdp')), may hold values from -3 to 3
- w_down: bfloat16 [3072, 768], P(('seq', 'fsdp')), may hold values from -0.21875 to 0.21875
- b_down: bfloat16 [768], P(('seq', 'fsdp')), may hold values from -3 to 3
Outputs:
- outputs: bfloat16 [32, 1024, 768], P('fsdp', 'seq')
- input_grad: float32 [32, 1024, 768], P('fsdp', 'seq')
- grad_first_gain: float32 [768], P(('seq', 'fsdp'))
- grad_first_shift: float32 [768], P(('seq', 'fsdp'))
- grad_w_qkv: float32 [768, 2304], P(('seq', 'fsdp'))
- grad_b_query: float32 [768], P(('seq', 'fsdp'))
- grad_b_value: float32 [768], P(('seq', 'fsdp'))
- grad_w_proj: float32 [768, 768], P(('seq', 'fsdp'))
- grad_b_proj: float32 [768], P(('seq', 'fsdp'))
- grad_second_gain: float32 [768], P(('seq', 'fsdp'))
- grad_second_shift: float32 [768], P(('seq', 'fsdp'))
- grad_w_up: float32 [768, 3072], P(('seq', 'fsdp'))
- grad_b_up: float32 [3072], P(('seq', 'fsdp'))
- grad_w_down: float32 [3072, 768], P(('seq', 'fsdp'))
- grad_b_down: float32 [768], P(('seq', 'fsdp'))
All inputs are finite; a program needn't handle non-finite values.
Results may differ from a plain program's by a relative error of at most 0.013.
Values may be sent and summed in bfloat16 or wider, within the bound.
No kernel may reach another device: no remote copies, remote signals or barrier semaphores. Data moves between devices by JAX's collectives and lax.ppermute only.
A program may use at most 192 MiB of HBM per device.

v0:
```python
import functools

import jax
import jax.numpy as jnp
from jax import lax
from jax.experimental import pallas as pl
from jax.experimental.pallas import tpu as pltpu
from jax.sharding import PartitionSpec as P

H = 12
HD = 64
PAIR = 2 * HD
EPSILON = 1e-05
F32 = jnp.float32
BF16 = jnp.bfloat16
NT = (((1,), (1,)), ((), ()))
NN = (((1,), (0,)), ((), ()))
SUB = 256
VMEM = 56 * 1024 * 1024


def dot(a, b, dims=NN):
    return lax.dot_general(a, b, dims, preferred_element_type=F32)


def head_lanes(x, head):
    lane = lax.broadcasted_iota(jnp.int32, x.shape, 1)
    return jnp.where((lane // HD) == head, x, jnp.zeros_like(x))


def masked(scores, start):
    key = lax.broadcasted_iota(jnp.int32, scores.shape, 0)
    query = lax.broadcasted_iota(jnp.int32, scores.shape, 1) + start
    return jnp.where(key <= query, scores, -1e30)


def forward_tile(q, k, v, causal):
    q = q * jnp.asarray(HD**-0.5, q.dtype)
    v_t = v.T
    rows, keys = q.shape[0], k.shape[0]
    outs, stats = [], []
    for head in range(2):
        q_h = head_lanes(q, head)
        v_h = v_t[head * HD : (head + 1) * HD]
        out_h, stat_h = [], []
        for start in range(0, rows, SUB):
            used = start + SUB if causal else keys
            s = dot(k[:used], q_h[start : start + SUB], NT)
            if causal:
                s = masked(s, start)
            top = jnp.max(s, axis=0, keepdims=True)
            e = jnp.exp(s - top)
            total = jnp.sum(e, axis=0, keepdims=True)
            out_h.append(dot(v_h[:, :used], e.astype(BF16)) / total)
            stat_h.append(top + jnp.log(total))
        outs.append(jnp.concatenate(out_h, axis=1))
        stats.append(jnp.concatenate(stat_h, axis=1))
    return jnp.concatenate(outs, axis=0).T, jnp.concatenate(stats, axis=0)


def backward_tile(q, k, v, g, stat, delta, causal):
    q = q * jnp.asarray(HD**-0.5, q.dtype)
    k_t = k.T
    rows, keys = q.shape[0], k.shape[0]
    dq_heads = []
    pieces = [None] * (keys // SUB), [None] * (keys // SUB)

    def add(which, start, value):
        for i in range(value.shape[0] // SUB):
            part = value[i * SUB : (i + 1) * SUB]
            old = pieces[which][start + i]
            pieces[which][start + i] = part if old is None else old + part

    for head in range(2):
        q_h = head_lanes(q, head)
        g_h = head_lanes(g, head)
        k_h = k_t[head * HD : (head + 1) * HD]
        dq_h = []
        for start in range(0, rows, SUB):
            used = start + SUB if causal else keys
            cols = slice(start, start + SUB)
            s = dot(k[:used], q_h[cols], NT)
            if causal:
                s = masked(s, start)
            p = jnp.exp(s - stat[head : head + 1, cols])
            dp = dot(v[:used], g_h[cols], NT)
            ds = (p * (dp - delta[head : head + 1, cols])).astype(BF16)
            add(1, 0, dot(p.astype(BF16), g_h[cols]))
            add(0, 0, dot(ds, q_h[cols]))
            dq_h.append(dot(k_h[:, :used], ds))
        dq_heads.append(jnp.concatenate(dq_h, axis=1))
    dq = jnp.concatenate(dq_heads, axis=0).T * HD**-0.5
    return dq, jnp.concatenate(pieces[0], axis=0), jnp.concatenate(pieces[1], axis=0)


def local_forward_kernel(q, k, v, o, stat):
    out, lse = forward_tile(q[0], k[0], v[0], True)
    o[0] = out.astype(BF16)
    stat[0, 0] = lse


def cross_forward_kernel(late, q, k, v, r1, r2, o, stat):
    is_late = late[0] == 1
    r = r1[0]
    out, lse = forward_tile(
        jnp.where(is_late, q[0], r),
        jnp.where(is_late, r, k[0]),
        jnp.where(is_late, r2[0], v[0]),
        False,
    )
    o[0] = out.astype(BF16)
    stat[0, 0] = lse


def spread(rows, size):
    a = jnp.broadcast_to(rows[0:1], (HD, size))
    b = jnp.broadcast_to(rows[1:2], (HD, size))
    return jnp.concatenate([a, b], axis=0).T


def merge_kernel(late, *refs):
    o, stat = refs[-2:]
    seqs, pairs = stat.shape[:2]
    is_late = late[0] == 1
    for b in range(seqs):
        o1, l1, o2, l2, o3, l3 = refs[6 * b : 6 * b + 6]
        for p in range(pairs):
            near = p < pairs // 2
            at = p if near else p - pairs // 2
            here = slice(p * PAIR, (p + 1) * PAIR)
            there = slice(at * PAIR, (at + 1) * PAIR)
            first = l1[0, p]
            second = (l2 if near else l3)[0, at]
            gap = second - first
            weight = jnp.where(is_late, 1.0 / (1.0 + jnp.exp(-gap)), 0.0)
            both = jnp.maximum(first, second) + jnp.log(1.0 + jnp.exp(-jnp.abs(gap)))
            stat[b, p] = jnp.where(is_late, both, first)
            own = o1[0, :, here].astype(F32)
            other = (o2 if near else o3)[0, :, there].astype(F32)
            o[b, :, here] = (own + spread(weight, own.shape[0]) * (other - own)).astype(BF16)


def local_backward_kernel(q, k, v, g, stat, delta, dq, dk, dv):
    a, b, c = backward_tile(q[0], k[0], v[0], g[0], stat[0, 0], delta[0, 0], True)
    dq[0] = a.astype(BF16)
    dk[0] = b.astype(BF16)
    dv[0] = c.astype(BF16)


def cross_backward_kernel(
    late, q, k, v, r1, r2, g, rg, stat, delta, rstat, rdelta, send, keep
):
    is_late = late[0] == 1
    r = r1[0]
    a, b, c = backward_tile(
        jnp.where(is_late, q[0], r),
        jnp.where(is_late, r, k[0]),
        jnp.where(is_late, r2[0], v[0]),
        jnp.where(is_late, g[0], rg[0]),
        jnp.where(is_late, stat[0, 0], rstat[0, 0, 0]),
        jnp.where(is_late, delta[0, 0], rdelta[0, 0, 0]),
        False,
    )
    a, b = a.astype(BF16), b.astype(BF16)
    place = pl.program_id(0) * PAIR
    span = pl.num_programs(0) * PAIR
    send[0, :, pl.ds(pl.multiple_of(place, PAIR), PAIR)] = jnp.where(is_late, b, a)
    send[0, :, pl.ds(pl.multiple_of(span + place, PAIR), PAIR)] = c.astype(BF16)
    keep[0] = jnp.where(is_late, a, b)


def cols(length, b0=0, shift=0, low=lambda p: p):
    return pl.BlockSpec((1, length, PAIR), lambda p: (b0, 0, low(p) + shift))


def stats(length, shift=0, low=lambda p: p):
    return pl.BlockSpec((1, 1, 2, length), lambda p: (0, low(p) + shift, 0, 0))


SCALAR = pl.BlockSpec(memory_space=pltpu.SMEM)


def skip(kernel, count, *refs):
    kernel(*refs[count:])


def call(kernel, grid, ins, outs, shapes, cost, name, scratch=(), after=()):
    body = functools.partial(skip, kernel, len(after)) if after else kernel
    made = pl.pallas_call(
        body,
        grid=grid,
        in_specs=[pl.BlockSpec(memory_space=pl.ANY)] * len(after) + list(ins),
        out_specs=outs,
        out_shape=shapes,
        scratch_shapes=scratch,
        compiler_params=pltpu.CompilerParams(vmem_limit_bytes=VMEM),
        cost_estimate=pl.CostEstimate(
            flops=cost, bytes_accessed=cost // 256, transcendentals=cost // 256
        ),
        name=name,
    )
    return functools.partial(made, *after)


def gelu_parts(u):
    c = (2.0 / jnp.pi) ** 0.5
    u2 = u * u
    t = jnp.tanh(u * (c + (c * 0.044715) * u2))
    half = 0.5 + 0.5 * t
    value = u * half
    slope = half + 0.5 * u * (1.0 - t * t) * (c + (3 * c * 0.044715) * u2)
    return value, slope


ROWS = 256


def column_sum(v):
    return jnp.sum(v, axis=0, keepdims=True)


def middle_kernel(
    x, att, w_proj, b_proj, gain, shift, dz, w_up, b_up, w_down, b_down,
    out, dm, d_att, delta, sums, g_across, g_bias, g_down,
    middle, a2, a2_t, z, d_a2, h_all, du_all,
):
    step = pl.program_id(0)
    last = pl.num_programs(0) - 1
    parts = [slice(i, i + ROWS) for i in range(0, x.shape[0], ROWS)]

    @pl.when(step == 0)
    def _():
        for part in parts:
            m = x[part].astype(F32) + (dot(att[part], w_proj[...]) + b_proj[...])
            middle[part] = m
            normal, _ = norm_parts(m)
            a2[part] = (normal * gain[...] + shift[...]).astype(BF16)
        a2_t[...] = a2[...].T
        z[...] = jnp.zeros_like(z)
        d_a2[...] = jnp.zeros_like(d_a2)

    @pl.when(step < last)
    def _():
        for part in parts:
            u = dot(a2[part], w_up[...]) + b_up[...]
            value, slope = gelu_parts(u)
            h = value.astype(BF16)
            h_all[part] = h
            z[part] += dot(h, w_down[...])
            du = (dot(dz[part], w_down[...], NT) * slope).astype(BF16)
            du_all[part] = du
            d_a2[part] += dot(du, w_up[...], NT)
        du = du_all[...]
        g_bias[...] = column_sum(du.astype(F32))
        g_across[...] = dot(a2_t[...], du).astype(BF16)
        g_down[...] = dot(h_all[...].T, dz[...]).astype(BF16)

    @pl.when(step == last)
    def _():
        total = [jnp.zeros((1, x.shape[1]), F32)] * 4
        length = delta.shape[-1]
        for part in parts:
            m = middle[part]
            out[part] = (m + (z[part] + b_down[...])).astype(BF16)
            normal, inv = norm_parts(m)
            grad = d_a2[part]
            scaled = grad * gain[...]
            back = scaled - jnp.mean(scaled, axis=-1, keepdims=True)
            back = back - normal * jnp.mean(scaled * normal, axis=-1, keepdims=True)
            dz32 = dz[part].astype(F32)
            d = dz32 + back * inv
            dm[part] = d
            dy = d.astype(BF16)
            a2[part] = dy
            d_o = dot(dy, w_proj[...], NT).astype(BF16)
            d_att[part] = d_o
            prod = (d_o.astype(F32) * att[part].astype(F32)).T
            b, first = divmod(part.start, length)
            for p in range(delta.shape[1]):
                heads = [prod[i * HD : (i + 1) * HD] for i in (2 * p, 2 * p + 1)]
                delta[b, p, :, first : first + ROWS] = jnp.concatenate(
                    [column_sum(h) for h in heads], axis=0
                )
            new = [grad * normal, grad, dy.astype(F32), dz32]
            total = [t + column_sum(n) for t, n in zip(total, new)]
        sums[...] = jnp.concatenate(total + total, axis=0)
        g_across[...] = dot(att[...].T, a2[...]).astype(BF16)


def middle_part(x, att, up_proj, b_proj, gain, shift, dz, b_up, w_down, b_down, seqs):
    tokens, width = x.shape
    hidden = b_up.shape[0]
    part = width
    steps = hidden // part
    row = lambda v: v.reshape(1, -1)
    once = lambda shape, col=0: pl.BlockSpec(
        shape, lambda j: (0, col), pipeline_mode=pl.Buffered(1)
    )
    act, vec = once((tokens, width)), once((1, width))
    kept = lambda shape: pl.BlockSpec(shape, lambda j: (0,) * len(shape))
    at = lambda j: jnp.minimum(j, steps - 1)
    across = pl.BlockSpec((width, part), lambda j: (0, at(j)))
    down = pl.BlockSpec((part, width), lambda j: (at(j), 0))
    bias = pl.BlockSpec((1, part), lambda j: (0, at(j)))
    delta = (seqs, width // PAIR, 2, tokens // seqs)
    return call(
        middle_kernel,
        (steps + 1,),
        [act, act, once((width, width), steps), vec, vec, vec, act]
        + [across, bias, down, vec],
        [kept((tokens, width))] * 3
        + [kept(delta), kept((8, width))]
        + [pl.BlockSpec((width, part), lambda j: (0, j)), bias, down],
        [
            jax.ShapeDtypeStruct((tokens, width), BF16),
            jax.ShapeDtypeStruct((tokens, width), F32),
            jax.ShapeDtypeStruct((tokens, width), BF16),
            jax.ShapeDtypeStruct(delta, F32),
            jax.ShapeDtypeStruct((8, width), F32),
            jax.ShapeDtypeStruct((width, hidden + width), BF16),
            jax.ShapeDtypeStruct((1, hidden), F32),
            jax.ShapeDtypeStruct((hidden, width), BF16),
        ],
        12 * tokens * width * hidden,
        "middle_part",
        [
            pltpu.VMEM((tokens, width), F32),
            pltpu.VMEM((tokens, width), BF16),
            pltpu.VMEM((width, tokens), BF16),
            pltpu.VMEM((tokens, width), F32),
            pltpu.VMEM((tokens, width), F32),
            pltpu.VMEM((tokens, part), BF16),
            pltpu.VMEM((tokens, part), BF16),
        ],
    )(
        x, att, up_proj, row(b_proj), row(gain), row(shift), dz,
        up_proj, row(b_up), w_down, row(b_down),
    )


def join_kernel(first, late, a1, *refs):
    seqs = (len(refs) - 4) // 6
    near, far = refs[: 3 * seqs], refs[3 * seqs : 6 * seqs]
    dp, g, sums, a1_t = refs[6 * seqs :]
    c = pl.program_id(0) + first
    is_late = late[0] == 1
    is_early = late[0] == 0
    use_keep = (is_late & (c == 0)) | (is_early & (c == 3))
    use_got = (is_late & (c == 1)) | (is_early & ((c == 2) | (c == 4)))
    use_send = is_early & (c == 5)

    @pl.when(c == first)
    def _():
        a1_t[...] = a1[...].T

    length = near[0].shape[1]
    for b in range(seqs):
        q, k, v = [r[0] for r in near[3 * b : 3 * b + 3]]
        send, keep, got = [r[0] for r in far[3 * b : 3 * b + 3]]
        base = jnp.where(c < 2, q, jnp.where(c < 4, k, v)).astype(F32)
        add = jnp.where(use_keep, keep, jnp.where(use_got, got, send)).astype(F32)
        add = jnp.where(use_keep | use_got | use_send, add, 0.0)
        dp[b * length : (b + 1) * length] = (base + add).astype(BF16)
    whole = dp[...]
    sums[...] = column_sum(whole.astype(F32))
    g[...] = dot(a1_t[...], whole).astype(BF16)


def join(late_ref, a1, near, far, first, count, after):
    tokens, width = a1.shape
    seqs = len(near)
    length, half = near[0][0].shape[1], width // 2
    shape = (1, length, half)
    third = [
        pl.BlockSpec(shape, lambda c, t=t: (0, 0, jnp.clip(c + first - 2 * t, 0, 1))) for t in range(3)
    ]
    away = [
        pl.BlockSpec(shape, lambda c: (0, 0, 1)),
        pl.BlockSpec(shape, lambda c: (0, 0, 0)),
        pl.BlockSpec(shape, lambda c: (0, 0, jnp.where(c + first < 3, 0, 1))),
    ]
    return call(
        functools.partial(join_kernel, first),
        (count,),
        [SCALAR, pl.BlockSpec((tokens, width), lambda c: (0, 0))] + third * seqs + away * seqs,
        [
            pl.BlockSpec((tokens, half), lambda c: (0, c)),
            pl.BlockSpec((width, half), lambda c: (0, c)),
            pl.BlockSpec((1, half), lambda c: (0, c)),
        ],
        [
            jax.ShapeDtypeStruct((tokens, count * half), BF16),
            jax.ShapeDtypeStruct((width, count * half), BF16),
            jax.ShapeDtypeStruct((1, count * half), F32),
        ],
        2 * tokens * width * count * half,
        f"join_{first}",
        [pltpu.VMEM((width, tokens), BF16)],
        after,
    )(late_ref, a1, *[r for n in near for r in n], *[r for f in far for r in f])


def input_kernel(x, dm, front, back, w, gain, out, sums):
    @pl.when(pl.program_id(0) == 0)
    def _():
        sums[...] = jnp.zeros_like(sums)

    cut = front.shape[1]
    grad = dot(front[...], w[:, :cut], NT) + dot(back[...], w[:, cut:], NT)
    normal, inv = norm_parts(x[...].astype(F32))
    scaled = grad * gain[...]
    part = scaled - jnp.mean(scaled, axis=-1, keepdims=True)
    part = part - normal * jnp.mean(scaled * normal, axis=-1, keepdims=True)
    out[...] = dm[...] + part * inv
    sums[0:1] += column_sum(grad * normal)
    sums[1:2] += column_sum(grad)


def input_part(x, dm, front, back, w, gain, after):
    tokens, width = x.shape
    block = lambda v: pl.BlockSpec((ROWS, v.shape[1]), lambda i: (i, 0))
    kept = lambda shape: pl.BlockSpec(shape, lambda i: (0, 0))
    return call(
        input_kernel,
        (tokens // ROWS,),
        [block(x), block(dm), block(front), block(back)]
        + [pl.BlockSpec(w.shape, lambda i: (0, 0), pipeline_mode=pl.Buffered(1))]
        + [kept((1, width))],
        [block(x), kept((8, width))],
        [jax.ShapeDtypeStruct((tokens, width), F32), jax.ShapeDtypeStruct((8, width), F32)],
        2 * tokens * width * w.shape[1],
        "input_part",
        after=after,
    )(x, dm, front, back, w, gain.reshape(1, width))


def nothing(*refs):
    pass


def tie(value, *others):
    anywhere = pl.BlockSpec(memory_space=pl.ANY)
    return pl.pallas_call(
        nothing,
        in_specs=[anywhere] * (1 + len(others)),
        out_specs=anywhere,
        out_shape=jax.ShapeDtypeStruct(value.shape, value.dtype),
        input_output_aliases={0: 0},
        name="tie",
    )(value, *others)


class Cube:
    def __init__(self):
        self.seq = lax.axis_size("seq")
        self.fsdp = lax.axis_size("fsdp")
        self.count = self.seq * self.fsdp
        self.bits = self.fsdp.bit_length() - 1
        place = lax.axis_index("fsdp")
        seq = lax.axis_index("seq")
        self.me = (seq * self.fsdp + place).astype(jnp.int32).reshape(1)
        self.mine = [seq] + [(place >> (self.bits - 1 - i)) & 1 for i in range(self.bits)]
        self.far = list(range(1, self.bits - 1))
        self.y = self.bits - 1
        self.core = self.bits
        self.x = 0

    def mask(self, dim):
        return self.fsdp if dim == 0 else 1 << (self.bits - dim)

    def swap(self, value, dim):
        if dim == 0:
            return lax.ppermute(value, "seq", [(i, i ^ 1) for i in range(self.seq)])
        flip = self.mask(dim)
        return lax.ppermute(value, "fsdp", [(i, i ^ flip) for i in range(self.fsdp)])


class Gather:
    def __init__(self, cube, block, order):
        self.cube, self.order, self.at = cube, order, 0
        self.value = block[None]

    def step(self, *after):
        other = self.cube.swap(self.value, self.order[self.at])
        if after:
            other = tie(other, *after)
        self.at += 1
        self.value = jnp.concatenate([self.value, other], axis=0)
        return self.value

    def last(self, *after):
        self.other = self.cube.swap(self.value, self.order[self.at])
        if after:
            self.other = tie(self.other, *after)
        return self


def place_kernel(masks, flips, cuts, me, *refs):
    count = len(masks)
    ins, outs = refs[: 2 * count], refs[2 * count :]

    def body(i, carry):
        for source, low, high, target, first in cuts:
            place = me[0]
            for k, mask in enumerate(masks[source]):
                place = place ^ (((i >> k) & 1) * mask)
            for other in range(2):
                outs[target][place ^ (other * flips[source]), :, first : first + high - low] = ins[
                    2 * source + other
                ][i, :, low:high]
        return carry

    lax.fori_loop(0, ins[0].shape[0], body, 0)


def assemble(cube, gathers, cuts, widths, name):
    masks = [[cube.mask(d) for d in g.order[:-1]] for g in gathers]
    flips = [cube.mask(g.order[-1]) for g in gathers]
    rows = gathers[0].value.shape[1]
    args = [item for g in gathers for item in (g.value, g.other)]
    out = pl.pallas_call(
        functools.partial(place_kernel, masks, flips, cuts),
        in_specs=[SCALAR] + [pl.BlockSpec(memory_space=pltpu.VMEM)] * len(args),
        out_specs=[pl.BlockSpec(memory_space=pltpu.VMEM)] * len(widths),
        out_shape=[jax.ShapeDtypeStruct((cube.count, rows, w), BF16) for w in widths],
        compiler_params=pltpu.CompilerParams(vmem_limit_bytes=VMEM),
        cost_estimate=pl.CostEstimate(
            flops=0, bytes_accessed=4 * cube.count * rows * sum(widths), transcendentals=0
        ),
        name=name,
    )(cube.me, *args)
    return [o.reshape(cube.count * rows, -1) for o in out]


class Scatter:
    def __init__(self, cube, whole, order, wire=BF16):
        self.cube, self.order, self.at, self.wire = cube, order, 0, wire
        self.rows, self.tail = whole.shape[0] // cube.count, whole.shape[1:]
        self.value = whole.reshape((2,) * (cube.bits + 1) + (self.rows,) + self.tail)
        self.send()

    def send(self):
        dim = self.order[self.at]
        own = self.cube.mine[dim]
        sent = lax.dynamic_index_in_dim(self.value, 1 - own, dim, keepdims=True)
        self.sent = sent.astype(self.wire)
        self.got = self.cube.swap(self.sent, dim)

    def join(self, other):
        self.tail = self.tail[:-1] + (self.tail[-1] + other.tail[-1],)
        self.value = jnp.concatenate([self.value, other.value], axis=-1)
        self.send()

    def step(self, *after, send=True):
        if self.at == len(self.order):
            return self.value
        dim = self.order[self.at]
        got = tie(self.got, *after) if after else self.got
        keep = lax.dynamic_index_in_dim(self.value, self.cube.mine[dim], dim, keepdims=True)
        self.at += 1
        self.value = keep.astype(F32) + got.astype(F32)
        if self.at <= 2:
            self.value = self.value.astype(self.wire)
        if self.at < len(self.order) and send:
            self.send()
        else:
            self.sent = self.value
        return self.sent

    def result(self):
        while self.at < len(self.order):
            self.step()
        return self.value.reshape((self.rows,) + self.tail)


def norm_parts(values):
    centre = values - jnp.mean(values, axis=-1, keepdims=True)
    spread_ = jnp.mean(centre * centre, axis=-1, keepdims=True)
    inv = lax.rsqrt(spread_ + EPSILON)
    return centre * inv, inv


def per_device(
    inputs,
    out_grad,
    first_gain,
    first_shift,
    w_qkv,
    b_query,
    b_value,
    w_proj,
    b_proj,
    second_gain,
    second_shift,
    w_up,
    b_up,
    w_down,
    b_down,
):
    cube = Cube()
    late = lax.axis_index("seq")
    late_ref = late.astype(jnp.int32).reshape(1)
    seqs, length, width = inputs.shape
    tokens = seqs * length
    rows = w_qkv.shape[0]
    half = width // 2
    pairs = width // PAIR

    small = [first_gain, first_shift, b_query, b_value, b_proj, second_gain, second_shift, b_down]
    flat = jnp.concatenate(small + [b_up])
    packed_small = jnp.pad(flat, (0, 128 * rows - flat.shape[0])).reshape(rows, 128)
    cut = 3 * half
    x_last = cube.far + [cube.y, cube.x, cube.core]
    y_last = cube.far + [cube.x, cube.y, cube.core]
    front = Gather(cube, w_qkv[:, :cut], x_last)
    back = Gather(cube, jnp.concatenate([w_qkv[:, cut:], packed_small], axis=1), y_last)
    hidden = w_up.shape[1]
    up_proj = lax.all_gather(
        jnp.concatenate([w_up, w_proj], axis=1), ("seq", "fsdp"), axis=0, tiled=True
    )
    down_full = lax.all_gather(w_down, ("seq", "fsdp"), axis=0, tiled=True)
    for _ in x_last[:-1]:
        front.step(), back.step()
    front.last(), back.last()
    qkv_full, table = assemble(
        cube,
        [front, back],
        [
            (0, 0, cut, 0, 0),
            (1, 0, 3 * width - cut, 0, cut),
            (1, 3 * width - cut, 3 * width - cut + 128, 1, 0),
        ],
        [3 * width, 128],
        "place_qkv",
    )
    lines = -(-flat.shape[0] // 128)
    table = table.reshape(cube.count, rows, 128)[:, :lines].astype(F32)
    table = table.reshape(cube.count, lines * 128)
    vectors = table[:, : 8 * rows].reshape(cube.count, 8, rows)
    vectors = vectors.transpose(1, 0, 2).reshape(8, width)
    (gain_one, shift_one, query_bias, value_bias, proj_bias, gain_two, shift_two, down_bias) = [
        vectors[i] for i in range(8)
    ]
    up_bias = table[:, 8 * rows : flat.shape[0]].reshape(-1)

    x = inputs.astype(F32).reshape(tokens, width)
    normal_one, inv_one = norm_parts(x)
    a1 = (normal_one * gain_one + shift_one).astype(BF16)
    bias = jnp.concatenate([query_bias, jnp.zeros((width,), F32), value_bias])
    packed = (dot(a1, qkv_full) + bias).astype(BF16).reshape(seqs, length, 3 * width)

    forth = [(0, 1)]
    back_way = [(1, 0)]
    both_ways = [(0, 1), (1, 0)]
    early = late == 0
    hp = pairs // 2
    tile = 2 * 2 * length * length * PAIR
    whole_shape = jax.ShapeDtypeStruct((1, length, width), BF16)
    half_shape = jax.ShapeDtypeStruct((1, length, half), BF16)
    stat_shape = jax.ShapeDtypeStruct((1, pairs, 2, length), F32)
    half_stat = jax.ShapeDtypeStruct((1, hp, 2, length), F32)
    one, st = cols(length), stats(length)

    def own(b, third, high=0):
        return cols(length, b, third * pairs + high * hp)

    def local_forward(b, data):
        return call(
            local_forward_kernel,
            (pairs,),
            [own(b, 0), own(b, 1), own(b, 2)],
            [one, st],
            [whole_shape, stat_shape],
            tile * pairs,
            f"local_forward_{b}",
        )(data, data, data)

    def cross_forward(b, r, after):
        return call(
            cross_forward_kernel,
            (hp,),
            [SCALAR, own(b, 0), own(b, 1, 1), own(b, 2, 1), one, cols(length, 0, hp)],
            [one, st],
            [half_shape, half_stat],
            tile * hp,
            f"cross_forward_{b}",
            after=after,
        )(late_ref, packed, packed, packed, r, r)

    arrived, local, cross = [], [], []
    for b in range(seqs):
        row = packed[b : b + 1]
        send = jnp.concatenate(
            [
                jnp.where(early, row[:, :, width : width + half], row[:, :, half:width]),
                row[:, :, 2 * width : 2 * width + half],
            ],
            axis=2,
        )
        arrived.append(lax.ppermute(send, "seq", both_ways))
    for b in range(seqs):
        local.append(local_forward(b, packed))
    after = (local[-1][0],)
    for b in range(seqs):
        o2, l2 = cross_forward(b, arrived[b], after)
        after = (o2,)
        o3, l3 = lax.ppermute(o2, "seq", forth), lax.ppermute(l2, "seq", forth)
        cross.append((o2, l2, o3, l3))
    flat = [item for b in range(seqs) for item in local[b] + cross[b]]
    attended, stat_all = pl.pallas_call(
        merge_kernel,
        in_specs=[SCALAR] + [pl.BlockSpec(memory_space=pltpu.VMEM)] * len(flat),
        out_specs=[pl.BlockSpec(memory_space=pltpu.VMEM)] * 2,
        out_shape=[
            jax.ShapeDtypeStruct((seqs, length, width), BF16),
            jax.ShapeDtypeStruct((seqs, pairs, 2, length), F32),
        ],
        compiler_params=pltpu.CompilerParams(vmem_limit_bytes=VMEM),
        name="merge",
    )(late_ref, *flat)
    o_flat = attended.reshape(tokens, width)
    dz = out_grad.reshape(tokens, width)
    outputs, dm, d_att, delta_all, sums_two, whole_across, sum_up, whole_down = middle_part(
        inputs.reshape(tokens, width),
        o_flat,
        up_proj,
        proj_bias,
        gain_two,
        shift_two,
        dz,
        up_bias,
        down_full,
        down_bias,
        seqs,
    )
    y_first, x_first = y_last[::-1], x_last[::-1]
    mixed = [cube.core] + cube.far[-1:] + [cube.y] + cube.far[:-1][::-1] + [cube.x]
    grad_down = Scatter(cube, whole_down, mixed)
    grad_across = Scatter(cube, whole_across, y_first)
    d_att = d_att.reshape(seqs, length, width)
    rg = [lax.ppermute(d_att[b : b + 1, :, half:], "seq", back_way) for b in range(seqs)]
    sent = jnp.stack([stat_all[:, hp:], delta_all[:, hp:]])
    sent = lax.ppermute(sent, "seq", back_way)
    st_of = lambda b: pl.BlockSpec((1, 1, 2, length), lambda p: (b, p, 0, 0))
    far_of = lambda i, b: pl.BlockSpec((1, 1, 1, 2, length), lambda p: (i, b, p, 0, 0))
    def local_backward(b, after):
        return call(
            local_backward_kernel,
            (pairs,),
            [own(b, 0), own(b, 1), own(b, 2), cols(length, b), st_of(b), st_of(b)],
            [one, one, one],
            [whole_shape] * 3,
            3 * tile * pairs,
            f"local_backward_{b}",
            after=after,
        )(packed, packed, packed, d_att, stat_all, delta_all)

    def cross_backward(b, r, g, after):
        return call(
            cross_backward_kernel,
            (hp,),
            [SCALAR, own(b, 0), own(b, 1, 1), own(b, 2, 1), one, cols(length, 0, hp)]
            + [cols(length, b), one, st_of(b), st_of(b), far_of(0, b), far_of(1, b)],
            [pl.BlockSpec((1, length, width), lambda p: (0, 0, 0)), one],
            [whole_shape, half_shape],
            3 * tile * hp,
            f"cross_backward_{b}",
            after=after,
        )(late_ref, packed, packed, packed, r, r, d_att, g, stat_all, delta_all, sent, sent)

    near_grads, far_grads = [], []
    after = (grad_down.sent, grad_across.sent)
    for b in range(seqs):
        near_grads.append(local_backward(b, after))
        moved = ()
        if b == 0:
            moved = grad_down.step(), grad_across.step()
        send, keep = cross_backward(b, arrived[b], rg[b], (near_grads[b][0],))
        far_grads.append((send, keep, lax.ppermute(send, "seq", both_ways)))
        after = (send,) + moved
    grad_down.step(), grad_across.step()
    dp_front, g_front, sums_front = join(late_ref, a1, near_grads, far_grads, 0, 3, ())
    grad_front = Scatter(cube, g_front, x_first)
    moved = grad_front.step()
    dp_back, g_back, sums_back = join(late_ref, a1, near_grads, far_grads, 3, 3, (moved,))
    grad_back = Scatter(cube, g_back, y_first)
    moved = grad_down.step(grad_back.sent), grad_across.step(grad_back.sent)
    moved = (grad_back.step(*moved),) + moved
    input_grad, sums_one = input_part(
        inputs.reshape(tokens, width), dm, dp_front, dp_back, qkv_full, gain_one, moved
    )
    moved = grad_front.step(sums_one), grad_back.step(sums_one)
    moved = grad_down.step(*moved), grad_across.step(*moved)
    grad_front.step(*moved, send=False), grad_back.step(*moved, send=False)
    grad_front.join(grad_back)
    sums = jnp.concatenate([sums_front[0], sums_back[0]])
    grads_small = [
        sums_one[0],
        sums_one[1],
        sums[:width],
        sums[2 * width :],
        sums_two[2],
        sums_two[0],
        sums_two[1],
        sums_two[3],
    ]
    devices = width // rows
    pack = jnp.concatenate(
        [item.reshape(devices, rows) for item in grads_small]
        + [sum_up.reshape(devices, -1)],
        axis=1,
    )
    pack = lax.all_to_all(pack, ("seq", "fsdp"), split_axis=0, concat_axis=0, tiled=True)
    pack = jnp.sum(pack, axis=0)
    parts = [pack[i * rows : (i + 1) * rows] for i in range(8)]
    g_up_bias = pack[8 * rows :]
    across = grad_across.result()
    return (
        outputs.reshape(seqs, length, width),
        input_grad.reshape(seqs, length, width),
        parts[0],
        parts[1],
        grad_front.result(),
        parts[2],
        parts[3],
        across[:, hidden:],
        parts[4],
        parts[5],
        parts[6],
        across[:, :hidden],
        g_up_bias,
        grad_down.result(),
        parts[7],
    )


def solution(mesh):
    vector, matrix = P(("seq", "fsdp")), P(("seq", "fsdp"), None)
    tokens = P("fsdp", "seq", None)
    placed = (
        tokens,
        tokens,
        vector,
        vector,
        matrix,
        vector,
        vector,
        matrix,
        vector,
        vector,
        vector,
        matrix,
        vector,
        matrix,
        vector,
    )
    return jax.shard_map(
        per_device, mesh=mesh, in_specs=placed, out_specs=placed, check_vma=False
    )
```

profile of v0, /device:TPU:0, one launch (start us, length us, event | category | flops | bytes accessed | tf_op | source)
XLA Modules:
  0.0 405.7 jit_solution(17718264659047595058)
XLA Ops:
  8.0 1.6 pad_maximum_fusion.6
  9.6 6.1 %concatenate.58 = bf16[288]{0:T(512)(128)(2,1)S(1)} concatenate(bf16[24]{0:T(256)(128)(2,1)} %param.17, bf16[24]{0:T(256)(128)(2,1)} %param.18, bf16[24]{0:T(256)(128)(2,1)} %param.20, bf16[24]{0:T(256)(128)(2,1)} %param.21, bf16[24]{0:T(256)(128)(2,1)} %param.23, bf16[24]{0:T(256)(128)(2,1)} %param.24, bf16[24]{0:T(256)(128)(2,1)} %param.25, bf16[24]{0:T(256)(128)(2,1)} %param.29, ...), dimensions={0} | concatenate | bytes 1152 | tf_op jit(solution)/shard_map/concatenate | solution.py:610
  16.6 4.1 %collective-permute-start.5 = (bf16[1,24,1280]{2,1,0:T(8,128)(2,1)S(1)}, bf16[1,24,1280]{2,1,0:T(8,128)(2,1)S(1)}, u32[]{:S(2)}, u32[]{:S(2)}) collective-permute-start(bf16[1,24,1280]{2,1,0:T(8,128)(2,1)S(1)} %maximum_bitcast_fusion), channel_id=1, source_target_pairs={{0,8},{1,9},{2,10},{3,11},{4,12},{5,13},{6,14},{7,15},{8,0},{9,1},... | collective-permute-start | bytes 184328 | tf_op jit(solution)/shard_map/ppermute | solution.py:475
  21.6 4.6 %collective-permute-done = bf16[1,24,1152]{2,1,0:T(8,128)(2,1)S(1)} collective-permute-done((bf16[1,24,1152]{2,1,0:T(8,128)(2,1)S(1)}, bf16[1,24,1152]{2,1,0:T(8,128)(2,1)S(1)}, u32[]{:S(2)}, u32[]{:S(2)}) %collective-permute-start) | collective-permute-done | bytes 55328 | tf_op jit(solution)/shard_map/ppermute | solution.py:475
  26.2 2.1 collective-permute-start.1
  28.4 4.8 %collective-permute-done.1 = bf16[2,24,1152]{2,1,0:T(8,128)(2,1)S(1)} collective-permute-done((bf16[2,24,1152]{2,1,0:T(8,128)(2,1)S(1)}, bf16[2,24,1152]{2,1,0:T(8,128)(2,1)S(1)}, u32[]{:S(2)}, u32[]{:S(2)}) %collective-permute-start.1) | collective-permute-done | bytes 110624 | tf_op jit(solution)/shard_map/ppermute | solution.py:475
  33.3 2.4 collective-permute-start.2
  36.1 1.4 collective-permute-start.7
  37.6 8.9 %collective-permute-done.7 = bf16[4,24,1280]{2,1,0:T(8,128)(2,1)S(1)} collective-permute-done((bf16[4,24,1280]{2,1,0:T(8,128)(2,1)S(1)}, bf16[4,24,1280]{2,1,0:T(8,128)(2,1)S(1)}, u32[]{:S(2)}, u32[]{:S(2)}) %collective-permute-start.7) | collective-permute-done | bytes 245792 | tf_op jit(solution)/shard_map/ppermute | solution.py:473
  46.9 2.5 collective-permute-start.3
  49.5 6.5 %collective-permute-done.8 = bf16[8,24,1280]{2,1,0:T(8,128)(2,1)S(1)} collective-permute-done((bf16[8,24,1280]{2,1,0:T(8,128)(2,1)S(1)}, bf16[8,24,1280]{2,1,0:T(8,128)(2,1)S(1)}, u32[]{:S(2)}, u32[]{:S(2)}) %collective-permute-start.8) | collective-permute-done | bytes 491552 | tf_op jit(solution)/shard_map/ppermute | solution.py:475
  56.1 1.4 collective-permute-done.3
  58.6 1.6 collective-permute-done.4.refs_1_
  60.2 4.6 %place_qkv.1 = (bf16[32,24,2304]{2,1,0:T(8,128)(2,1)}, bf16[32,24,128]{2,1,0:T(8,128)(2,1)}) custom-call(s32[1]{0:T(128)} %bitcast.2.me, bf16[16,24,1152]{2,1,0:T(8,128)(2,1)} %copy-done.31, bf16[16,24,1152]{2,1,0:T(8,128)(2,1)} %collective-permute-done.4.refs_1_, bf16[16,24,1280]{2,1,0:T(8,128)(2,1)} %copy-done.30, ...), custom_call_target="tpu_custom_call" | custom-call | bytes 7471104 | tf_op jit(solution)/shard_map/place_qkv/pallas_call | solution.py:521
  67.2 6.1 %add_convert_fusion = bf16[1024,2304]{1,0:T(8,128)(2,1)S(1)} fusion(bf16[1024,768]{1,0:T(8,128)(2,1)S(1)} %bitcast.104, bf16[768,2304]{1,0:T(8,128)(2,1)} %bitcast.112, f32[2304]{0:T(1024)S(1)} %pad_maximum_fusion.10), kind=kOutput, calls=%fused_computation | convolution fusion | flops 3628597248 | bytes 9839616 | tf_op jit(solution)/shard_map/dot_general | solution.py:23
  73.6 1.8 copy-done
  75.5 1.7 collective-permute-start.10
  77.9 10.6 %local_forward_1.1 = (bf16[1,512,768]{2,1,0:T(8,128)(2,1)}, f32[1,6,2,512]{3,2,1,0:T(2,128)}) custom-call(bf16[2,512,2304]{2,1,0:T(8,128)(2,1)} %bitcast.63, bf16[2,512,2304]{2,1,0:T(8,128)(2,1)} %bitcast.64, bf16[2,512,2304]{2,1,0:T(8,128)(2,1)} %bitcast.65), custom_call_target="tpu_custom_call" | custom-call | flops 805306368 | bytes 3145728 | tf_op jit(solution)/shard_map/local_forward_1/pallas_call | solution.py:668
  88.4 8.9 %collective-permute-done.10.refs_5_.refs_6_ = bf16[1,512,768]{2,1,0:T(8,128)(2,1)S(1)} collective-permute-done((bf16[1,512,768]{2,1,0:T(8,128)(2,1)S(1)}, bf16[1,512,768]{2,1,0:T(8,128)(2,1)S(1)}, u32[]{:S(2)}, u32[]{:S(2)}) %collective-permute-start.10) | collective-permute-done | bytes 786464 | tf_op jit(solution)/shard_map/ppermute | solution.py:700
  98.2 7.7 %cross_forward_0.1 = (bf16[1,512,384]{2,1,0:T(8,128)(2,1)}, f32[1,3,2,512]{3,2,1,0:T(2,128)}) custom-call(bf16[1,512,768]{2,1,0:T(8,128)(2,1)} %get-tuple-element.57.refs_0_.refs_6_, s32[1]{0:T(128)} %bitcast.1.refs_1_.late, bf16[2,512,2304]{2,1,0:T(8,128)(2,1)} %bitcast.66, bf16[2,512,2304]{2,1,0:T(8,128)(2,1)} %bitcast.67, bf16[2,512,2304]{2,1,0:T(8,128)(2,1)} %bitcast.68, ...), custom_call_target="tpu_custom_call" | custom-call | flops 402653184 | bytes 1572864 | tf_op jit(solution)/shard_map/cross_forward_0/pallas_call | solution.py:679
  105.9 10.6 %collective-permute-done.13.refs_5_.refs_6_ = bf16[1,512,768]{2,1,0:T(8,128)(2,1)S(1)} collective-permute-done((bf16[1,512,768]{2,1,0:T(8,128)(2,1)S(1)}, bf16[1,512,768]{2,1,0:T(8,128)(2,1)S(1)}, u32[]{:S(2)}, u32[]{:S(2)}) %collective-permute-start.13) | collective-permute-done | bytes 786464 | tf_op jit(solution)/shard_map/ppermute | solution.py:700
  117.4 7.8 %cross_forward_1.1 = (bf16[1,512,384]{2,1,0:T(8,128)(2,1)}, f32[1,3,2,512]{3,2,1,0:T(2,128)}) custom-call(bf16[1,512,384]{2,1,0:T(8,128)(2,1)} %get-tuple-element.58.refs_0_.refs_2_, s32[1]{0:T(128)} %bitcast.1.refs_1_.late, bf16[2,512,2304]{2,1,0:T(8,128)(2,1)} %bitcast.69, bf16[2,512,2304]{2,1,0:T(8,128)(2,1)} %bitcast.70, bf16[2,512,2304]{2,1,0:T(8,128)(2,1)} %bitcast.71, ...), custom_call_target="tpu_custom_call" | custom-call | flops 402653184 | bytes 1572864 | tf_op jit(solution)/shard_map/cross_forward_1/pallas_call | solution.py:679
  125.1 4.4 %collective-permute-start.14 = (bf16[1,512,384]{2,1,0:T(8,128)(2,1)}, bf16[1,512,384]{2,1,0:T(8,128)(2,1)S(1)}, u32[]{:S(2)}, u32[]{:S(2)}) collective-permute-start(bf16[1,512,384]{2,1,0:T(8,128)(2,1)} %get-tuple-element.61.refs_8_), channel_id=1, source_target_pairs={{0,16},{1,17},{2,18},{3,19},{4,20},{5,21},{6,22},{7,23},{8,24},{9,... | collective-permute-start | bytes 1179656 | tf_op jit(solution)/shard_map/ppermute | solution.py:707
  133.5 10.6 %local_forward_0.1 = (bf16[1,512,768]{2,1,0:T(8,128)(2,1)}, f32[1,6,2,512]{3,2,1,0:T(2,128)}) custom-call(bf16[2,512,2304]{2,1,0:T(8,128)(2,1)} %bitcast.74, bf16[2,512,2304]{2,1,0:T(8,128)(2,1)} %bitcast.73, bf16[2,512,2304]{2,1,0:T(8,128)(2,1)} %bitcast.72), custom_call_target="tpu_custom_call" | custom-call | flops 805306368 | bytes 3145728 | tf_op jit(solution)/shard_map/local_forward_0/pallas_call | solution.py:668
  147.5 7.7 %collective-permute-done.15.refs_11_ = f32[1,3,2,512]{3,2,1,0:T(2,128)S(1)} collective-permute-done((f32[1,3,2,512]{3,2,1,0:T(2,128)}, f32[1,3,2,512]{3,2,1,0:T(2,128)S(1)}, u32[]{:S(2)}, u32[]{:S(2)}) %collective-permute-start.15) | collective-permute-done | bytes 12320 | tf_op jit(solution)/shard_map/ppermute | solution.py:707
  156.3 4.0 merge.1
  160.3 56.6 %middle_part.1 = (bf16[1024,768]{1,0:T(8,128)(2,1)}, f32[1024,768]{1,0:T(8,128)}, bf16[1024,768]{1,0:T(8,128)(2,1)}, f32[2,6,2,512]{3,2,1,0:T(2,128)}, f32[8,768...) custom-call(bf16[1024,768]{1,0:T(8,128)(2,1)} %bitcast.92, ...), custom_call_target="tpu_custom_call" | custom-call | flops 28991029248 | bytes 113246208 | tf_op jit(solution)/shard_map/middle_part/pallas_call | solution.py:306
  217.0 3.8 constant_dynamic-slice_fusion.10.refs_1_
  220.8 1.6 constant_dynamic-slice_fusion.11.refs_0_
  224.5 1.4 collective-permute-start.16
  226.0 1.4 collective-permute-start.17
  227.4 10.4 %local_backward_0.1 = (bf16[1,512,768]{2,1,0:T(8,128)(2,1)}, bf16[1,512,768]{2,1,0:T(8,128)(2,1)}, bf16[1,512,768]{2,1,0:T(8,128)(2,1)}) custom-call(bf16[2,2,2,2,1,96,768]{6,5,4,3,2,1,0:T(8,128)(2,1)} %constant_dynamic-slice_fusion.11.refs_0_, bf16[2,2,2,2,1,24,3840]{6,5,4,3,2,1,0:T(8,128)(2,1)} %constant_dynamic-slice_fusion.10.refs_1_, ...), custom_call_target="tpu_custom_call" | custom-call | flops 2415919104 | bytes 9437184 | tf_op jit(solution)/shard_map/local_backward_0/pallas_call | solution.py:747
  239.2 2.8 collective-permute-done.17.refs_11_.refs_12_
  242.8 7.2 %cross_backward_0.1 = (bf16[1,512,768]{2,1,0:T(8,128)(2,1)}, bf16[1,512,384]{2,1,0:T(8,128)(2,1)}) custom-call(bf16[1,512,768]{2,1,0:T(8,128)(2,1)} %get-tuple-element.70.refs_0_.refs_3_, s32[1]{0:T(128)} %bitcast.1.refs_1_.late, bf16[2,512,2304]{2,1,0:T(8,128)(2,1)} %bitcast.78, bf16[2,512,2304]{2,1,0:T(8,128)(2,1)} %bitcast.79, ...), custom_call_target="tpu_custom_call" | custom-call | flops 1207959552 | bytes 4718592 | tf_op jit(solution)/shard_map/cross_backward_0/pallas_call | solution.py:759
  249.9 3.5 collective-permute-start.20
  253.5 2.4 add_convert_fusion.2
  255.9 1.8 collective-permute-start.25
  257.7 3.4 add_convert_fusion.1
  261.1 1.6 copy-done.6
  264.0 1.6 collective-permute-start.27
  265.6 10.5 %local_backward_1.1 = (bf16[1,512,768]{2,1,0:T(8,128)(2,1)}, bf16[1,512,768]{2,1,0:T(8,128)(2,1)}, bf16[1,512,768]{2,1,0:T(8,128)(2,1)}) custom-call(bf16[1,512,768]{2,1,0:T(8,128)(2,1)} %get-tuple-element.73.refs_0_.refs_6_.refs_9_, bf16[2,2,1,2,1,96,768]{6,5,4,3,2,1,0:T(8,128)(2,1)} %copy-done.11, ...), custom_call_target="tpu_custom_call" | custom-call | flops 2415919104 | bytes 9437184 | tf_op jit(solution)/shard_map/local_backward_1/pallas_call | solution.py:747
  276.1 7.3 %cross_backward_1.1 = (bf16[1,512,768]{2,1,0:T(8,128)(2,1)}, bf16[1,512,384]{2,1,0:T(8,128)(2,1)}) custom-call(bf16[1,512,768]{2,1,0:T(8,128)(2,1)} %get-tuple-element.74.refs_0_.refs_3_.refs_6_, s32[1]{0:T(128)} %bitcast.1.refs_1_.late, bf16[2,512,2304]{2,1,0:T(8,128)(2,1)} %bitcast.84, bf16[2,512,2304]{2,1,0:T(8,128)(2,1)} %bitcast.85, ...), custom_call_target="tpu_custom_call" | custom-call | flops 1207959552 | bytes 4718592 | tf_op jit(solution)/shard_map/cross_backward_1/pallas_call | solution.py:759
  283.5 1.8 fusion.3.a1.refs_2_
  291.3 2.0 reduce.56
  293.3 1.4 reshape.202
  294.7 1.6 add_convert_fusion.5
  297.7 4.9 %collective-permute-done.22.refs_11_.refs_14_ = bf16[1,512,768]{2,1,0:T(8,128)(2,1)} collective-permute-done((bf16[1,512,768]{2,1,0:T(8,128)(2,1)}, bf16[1,512,768]{2,1,0:T(8,128)(2,1)}, u32[]{:S(2)}, u32[]{:S(2)}) %collective-permute-start.22) | collective-permute-done | bytes 786464 | tf_op jit(solution)/shard_map/ppermute | solution.py:779
  302.6 8.3 %join_0.1 = (bf16[1024,1152]{1,0:T(8,128)(2,1)}, bf16[768,1152]{1,0:T(8,128)(2,1)}, f32[1,1152]{1,0:T(1,128)}) custom-call(s32[1]{0:T(128)} %bitcast.1.refs_1_.late, bf16[1024,768]{1,0:T(8,128)(2,1)} %fusion.3.a1.refs_2_, bf16[1,512,768]{2,1,0:T(8,128)(2,1)} %get-tuple-element.70.refs_0_.refs_3_, bf16[1,512,768]{2,1,0:T(8,128)(2,1)} %get-tuple-element.71.refs_1_.refs_4_, ...), custom_call_target="tpu_custom_call" | custom-call | flops 1811939328 | bytes 7077888 | tf_op jit(solution)/shard_map/join_0/pallas_call | solution.py:382
  310.9 2.2 constant_dynamic-slice_fusion.7
  314.5 1.8 add_convert_fusion.4
  317.7 1.4 add_convert_fusion.7
  320.8 1.7 collective-permute-start.29
  322.5 8.1 %join_3.1 = (bf16[1024,1152]{1,0:T(8,128)(2,1)}, bf16[768,1152]{1,0:T(8,128)(2,1)}, f32[1,1152]{1,0:T(1,128)}) custom-call(bf16[1,2,2,2,1,24,1152]{6,5,4,3,2,1,0:T(8,128)(2,1)} %constant_dynamic-slice_fusion.6.refs_0_, s32[1]{0:T(128)} %bitcast.1.refs_1_.late, bf16[1024,768]{1,0:T(8,128)(2,1)} %fusion.3.a1.refs_2_, ...), custom_call_target="tpu_custom_call" | custom-call | flops 1811939328 | bytes 7077888 | tf_op jit(solution)/shard_map/join_3/pallas_call | solution.py:382
  341.5 1.4 collective-permute-start.33
  343.0 1.4 add_convert_fusion.6
  345.8 10.2 %input_part.1 = (f32[1024,768]{1,0:T(8,128)}, f32[8,768]{1,0:T(8,128)}) custom-call(bf16[2,2,2,1,1,24,1152]{6,5,4,3,2,1,0:T(8,128)(2,1)} %constant_dynamic-slice_fusion.2.refs_0_, bf16[2,1,1,1,1,96,768]{6,5,4,3,2,1,0:T(8,128)(2,1)} %dynamic-slice_convert_fusion.1.refs_1_, bf16[1,2,1,1,1,24,3840]{6,5,4,3,2,1,0:T(8,128)(2,1)} %dynamic-slice_convert_fusion.refs_2_, ...), custom_call_target="tpu_custom_call" | custom-call | flops 3623878656 | bytes 14155776 | tf_op jit(solution)/shard_map/input_part/pallas_call | solution.py:423
  359.0 3.4 all-to-all-start
  363.1 1.8 collective-permute-start.30
  364.9 5.0 %all-to-all-done = f32[32,1,288]{2,1,0:T(1,128)S(1)} async-done(((f32[32,1,288]{2,1,0:T(1,128)}), f32[32,1,288]{2,1,0:T(1,128)S(1)}, u32[]{:S(2)}, u32[]{:S(2)}) %all-to-all-start) | async-done | bytes 36896 | tf_op jit(solution)/shard_map/all_to_all | solution.py:813
  375.4 1.4 collective-permute-start.38
  379.6 1.9 collective-permute-done.34.refs_0_
  383.7 1.7 add_bitcast_fusion.1
  385.4 6.6 %collective-permute-done.35 = bf16[1,2,1,1,1,24,2304]{6,5,4,3,2,1,0:T(8,128)(2,1)S(1)} collective-permute-done((bf16[1,2,1,1,1,24,2304]{6,5,4,3,2,1,0:T(8,128)(2,1)S(1)}, bf16[1,2,1,1,1,24,2304]{6,5,4,3,2,1,0:T(8,128)(2,1)S(1)}, u32[]{:S(2)}, u32[]{:S(2)}) %collective-permute-start.35) | collective-permute-done | bytes 221216 | tf_op jit(solution)/shard_map/ppermute | solution.py:475
  393.6 4.4 %collective-permute-done.36 = bf16[1,1,1,1,1,24,2304]{6,5,4,3,2,1,0:T(8,128)(2,1)S(1)} collective-permute-done((bf16[1,1,1,1,1,24,2304]{6,5,4,3,2,1,0:T(8,128)(2,1)S(1)}, bf16[1,1,1,1,1,24,2304]{6,5,4,3,2,1,0:T(8,128)(2,1)S(1)}, u32[]{:S(2)}, u32[]{:S(2)}) %collective-permute-start.36) | collective-permute-done | bytes 110624 | tf_op jit(solution)/shard_map/ppermute | solution.py:475
  (261 shorter events, 64.7 us)
Async XLA Ops:
  7.2 153.1 %all-gather.5.cloned.1.call-start = ((), (), s32[]{:S(2)}) async-start(), calls=%async_computation.2 | async-start | bytes 4866048 | tf_op jit(solution)/shard_map/all_gather | solution.py:621
  7.9 152.4 %all-gather.3.cloned.1.call-start = ((), (), s32[]{:S(2)}) async-start(), calls=%async_computation.1 | async-start | bytes 6082560 | tf_op jit(solution)/shard_map/all_gather | solution.py:618
  16.6 11.7 %collective-permute-start.5 = (bf16[1,24,1280]{2,1,0:T(8,128)(2,1)S(1)}, bf16[1,24,1280]{2,1,0:T(8,128)(2,1)S(1)}, u32[]{:S(2)}, u32[]{:S(2)}) collective-permute-start(bf16[1,24,1280]{2,1,0:T(8,128)(2,1)S(1)} %maximum_bitcast_fusion), channel_id=1, source_target_pairs={{0,8},{1,9},{2,10},{3,11},{4,12},{5,13},{6,14},{7,15},{8,0},{9,1},... | collective-permute-start | bytes 184328 | tf_op jit(solution)/shard_map/ppermute | solution.py:475
  20.7 5.5 %collective-permute-start = (bf16[1,24,1152]{2,1,0:T(8,128)(2,1)S(1)}, bf16[1,24,1152]{2,1,0:T(8,128)(2,1)S(1)}, u32[]{:S(2)}, u32[]{:S(2)}) collective-permute-start(bf16[1,24,1152]{2,1,0:T(8,128)(2,1)S(1)} %get-tuple-element.115), channel_id=1, source_target_pairs={{0,8},{1,9},{2,10},{3,11},{4,12},{5,13},{6,14},{7,15},{8,0},{9,1},... | collective-permute-start | bytes 165896 | tf_op jit(solution)/shard_map/ppermute | solution.py:475
  26.2 7.1 %collective-permute-start.1 = (bf16[2,24,1152]{2,1,0:T(8,128)(2,1)S(1)}, bf16[2,24,1152]{2,1,0:T(8,128)(2,1)S(1)}, u32[]{:S(2)}, u32[]{:S(2)}) collective-permute-start(bf16[2,24,1152]{2,1,0:T(8,128)(2,1)S(1)} %pad_maximum_fusion.8), channel_id=1, source_target_pairs={{0,4},{1,5},{2,6},{3,7},{4,0},{5,1},{6,2},{7,3},{8,12},{9,13},{10,... | collective-permute-start | bytes 331784 | tf_op jit(solution)/shard_map/ppermute | solution.py:475
  28.3 7.7 %collective-permute-start.6 = (bf16[2,24,1280]{2,1,0:T(8,128)(2,1)S(1)}, bf16[2,24,1280]{2,1,0:T(8,128)(2,1)S(1)}, u32[]{:S(2)}, u32[]{:S(2)}) collective-permute-start(bf16[2,24,1280]{2,1,0:T(8,128)(2,1)S(1)} %pad_maximum_fusion.7), channel_id=1, source_target_pairs={{0,4},{1,5},{2,6},{3,7},{4,0},{5,1},{6,2},{7,3},{8,12},{9,13},{10,... | collective-permute-start | bytes 368648 | tf_op jit(solution)/shard_map/ppermute | solution.py:475
  33.3 13.5 %collective-permute-start.2 = (bf16[4,24,1152]{2,1,0:T(8,128)(2,1)S(1)}, bf16[4,24,1152]{2,1,0:T(8,128)(2,1)S(1)}, u32[]{:S(2)}, u32[]{:S(2)}) collective-permute-start(bf16[4,24,1152]{2,1,0:T(8,128)(2,1)S(1)} %pad_maximum_fusion.5), channel_id=1, source_target_pairs={{0,2},{1,3},{2,0},{3,1},{4,6},{5,7},{6,4},{7,5},{8,10},{9,11},{10,... | collective-permute-start | bytes 663560 | tf_op jit(solution)/shard_map/ppermute | solution.py:475
  36.1 10.3 %collective-permute-start.7 = (bf16[4,24,1280]{2,1,0:T(8,128)(2,1)S(1)}, bf16[4,24,1280]{2,1,0:T(8,128)(2,1)S(1)}, u32[]{:S(2)}, u32[]{:S(2)}) collective-permute-start(bf16[4,24,1280]{2,1,0:T(8,128)(2,1)S(1)} %pad_maximum_fusion.4), channel_id=1, source_target_pairs={{0,16},{16,0},{1,17},{17,1},{2,18},{18,2},{3,19},{19,3},{4,20},{20... | collective-permute-start | bytes 737288 | tf_op jit(solution)/shard_map/ppermute | solution.py:473
  37.6 20.1 %copy-start.2 = (bf16[2,512,768]{2,1,0:T(8,128)(2,1)S(1)}, bf16[2,512,768]{2,1,0:T(8,128)(2,1)}, u32[]{:S(2)}) copy-start(bf16[2,512,768]{2,1,0:T(8,128)(2,1)} %param.15) | copy-start | bytes 4718596
  46.5 9.5 %collective-permute-start.8 = (bf16[8,24,1280]{2,1,0:T(8,128)(2,1)S(1)}, bf16[8,24,1280]{2,1,0:T(8,128)(2,1)S(1)}, u32[]{:S(2)}, u32[]{:S(2)}) collective-permute-start(bf16[8,24,1280]{2,1,0:T(8,128)(2,1)S(1)} %pad_maximum_fusion.2), channel_id=1, source_target_pairs={{0,2},{1,3},{2,0},{3,1},{4,6},{5,7},{6,4},{7,5},{8,10},{9,11},{10,... | collective-permute-start | bytes 1474568 | tf_op jit(solution)/shard_map/ppermute | solution.py:475
  46.9 10.6 %collective-permute-start.3 = (bf16[8,24,1152]{2,1,0:T(8,128)(2,1)S(1)}, bf16[8,24,1152]{2,1,0:T(8,128)(2,1)S(1)}, u32[]{:S(2)}, u32[]{:S(2)}) collective-permute-start(bf16[8,24,1152]{2,1,0:T(8,128)(2,1)S(1)} %pad_maximum_fusion.3), channel_id=1, source_target_pairs={{0,16},{16,0},{1,17},{17,1},{2,18},{18,2},{3,19},{19,3},{4,20},{20... | collective-permute-start | bytes 1327112 | tf_op jit(solution)/shard_map/ppermute | solution.py:473
  56.0 4.2 %copy-start.30 = (bf16[16,24,1280]{2,1,0:T(8,128)(2,1)}, bf16[16,24,1280]{2,1,0:T(8,128)(2,1)S(1)}, u32[]{:S(2)}) copy-start(bf16[16,24,1280]{2,1,0:T(8,128)(2,1)S(1)} %constant_dynamic-update-slice_fusion.5.refs_2_) | copy-start | bytes 2949124
  56.0 4.2 %collective-permute-start.9 = (bf16[16,24,1280]{2,1,0:T(8,128)(2,1)S(1)}, bf16[16,24,1280]{2,1,0:T(8,128)(2,1)}, u32[]{:S(2)}, u32[]{:S(2)}) collective-permute-start(bf16[16,24,1280]{2,1,0:T(8,128)(2,1)S(1)} %constant_dynamic-update-slice_fusion.5.refs_2_), channel_id=1, source_target_pairs={{0,1},{1,0},{2,3},{3,2},{4,5},{5,4},{6,7},{7,6},{8,9},{9,8},{10,11... | collective-permute-start | bytes 2949128 | tf_op jit(solution)/shard_map/ppermute | solution.py:475
  57.6 2.6 collective-permute-start.4
  75.5 21.7 %collective-permute-start.10 = (bf16[1,512,768]{2,1,0:T(8,128)(2,1)S(1)}, bf16[1,512,768]{2,1,0:T(8,128)(2,1)S(1)}, u32[]{:S(2)}, u32[]{:S(2)}) collective-permute-start(bf16[1,512,768]{2,1,0:T(8,128)(2,1)S(1)} %pad_maximum_fusion), channel_id=1, source_target_pairs={{0,16},{16,0},{1,17},{17,1},{2,18},{18,2},{3,19},{19,3},{4,20},{20... | collective-permute-start | bytes 2359304 | tf_op jit(solution)/shard_map/ppermute | solution.py:700
  77.4 39.1 %collective-permute-start.13 = (bf16[1,512,768]{2,1,0:T(8,128)(2,1)S(1)}, bf16[1,512,768]{2,1,0:T(8,128)(2,1)S(1)}, u32[]{:S(2)}, u32[]{:S(2)}) collective-permute-start(bf16[1,512,768]{2,1,0:T(8,128)(2,1)S(1)} %pad_maximum_fusion.1), channel_id=1, source_target_pairs={{0,16},{16,0},{1,17},{17,1},{2,18},{18,2},{3,19},{19,3},{4,20},{20... | collective-permute-start | bytes 2359304 | tf_op jit(solution)/shard_map/ppermute | solution.py:700
  117.4 12.2 %copy-start.29 = (bf16[1,512,384]{2,1,0:T(8,128)(2,1)S(1)}, bf16[1,512,384]{2,1,0:T(8,128)(2,1)}, u32[]{:S(2)}) copy-start(bf16[1,512,384]{2,1,0:T(8,128)(2,1)} %get-tuple-element.58.refs_0_.refs_2_) | copy-start | bytes 1179652
  117.4 14.8 %copy-start.44 = (f32[1,3,2,512]{3,2,1,0:T(2,128)S(1)}, f32[1,3,2,512]{3,2,1,0:T(2,128)}, u32[]{:S(2)}) copy-start(f32[1,3,2,512]{3,2,1,0:T(2,128)} %get-tuple-element.59.refs_3_) | copy-start | bytes 36868
  125.1 30.3 %collective-permute-start.14 = (bf16[1,512,384]{2,1,0:T(8,128)(2,1)}, bf16[1,512,384]{2,1,0:T(8,128)(2,1)S(1)}, u32[]{:S(2)}, u32[]{:S(2)}) collective-permute-start(bf16[1,512,384]{2,1,0:T(8,128)(2,1)} %get-tuple-element.61.refs_8_), channel_id=1, source_target_pairs={{0,16},{1,17},{2,18},{3,19},{4,20},{5,21},{6,22},{7,23},{8,24},{9,... | collective-permute-start | bytes 1179656 | tf_op jit(solution)/shard_map/ppermute | solution.py:707
  129.5 25.8 %collective-permute-start.11 = (bf16[1,512,384]{2,1,0:T(8,128)(2,1)S(1)}, bf16[1,512,384]{2,1,0:T(8,128)(2,1)S(1)}, u32[]{:S(2)}, u32[]{:S(2)}) collective-permute-start(bf16[1,512,384]{2,1,0:T(8,128)(2,1)S(1)} %copy-done.29), channel_id=1, source_target_pairs={{0,16},{1,17},{2,18},{3,19},{4,20},{5,21},{6,22},{7,23},{8,24},{9,... | collective-permute-start | bytes 1179656 | tf_op jit(solution)/shard_map/ppermute | solution.py:707
  130.9 24.4 %collective-permute-start.15 = (f32[1,3,2,512]{3,2,1,0:T(2,128)}, f32[1,3,2,512]{3,2,1,0:T(2,128)S(1)}, u32[]{:S(2)}, u32[]{:S(2)}) collective-permute-start(f32[1,3,2,512]{3,2,1,0:T(2,128)} %get-tuple-element.62.refs_9_), channel_id=1, source_target_pairs={{0,16},{1,17},{2,18},{3,19},{4,20},{5,21},{6,22},{7,23},{8,24},{9,... | collective-permute-start | bytes 36872 | tf_op jit(solution)/shard_map/ppermute | solution.py:707
  132.2 23.2 %collective-permute-start.12 = (f32[1,3,2,512]{3,2,1,0:T(2,128)S(1)}, f32[1,3,2,512]{3,2,1,0:T(2,128)S(1)}, u32[]{:S(2)}, u32[]{:S(2)}) collective-permute-start(f32[1,3,2,512]{3,2,1,0:T(2,128)S(1)} %copy-done.44), channel_id=1, source_target_pairs={{0,16},{1,17},{2,18},{3,19},{4,20},{5,21},{6,22},{7,23},{8,24},{9,... | collective-permute-start | bytes 36872 | tf_op jit(solution)/shard_map/ppermute | solution.py:707
  220.8 36.9 %collective-permute-start.19 = (bf16[2,2,2,2,1,24,3840]{6,5,4,3,2,1,0:T(8,128)(2,1)}, bf16[2,2,2,2,1,24,3840]{6,5,4,3,2,1,0:T(8,128)(2,1)}, u32[]{:S(2)}, u32[]{:S(2)}) collective-permute-start(bf16[2,2,2,2,1,24,3840]{6,5,4,3,2,1,0:T(8,128)(2,1)} %constant_dynamic-slice_fusion.10.refs_1_), channel_id=1, source_target_pairs={{0,1},{1,0},{2,3},{3,2},{4,5},{5,4},{6,7},{7,6},{8,9},{9,8},{10,11... | collective-permute-start | bytes 8847368 | tf_op jit(solution)/shard_map/ppermute | solution.py:475
  220.8 5.2 %copy-start.33 = (f32[2,6,2,512]{3,2,1,0:T(2,128)S(1)}, f32[2,6,2,512]{3,2,1,0:T(2,128)}, u32[]{:S(2)}) copy-start(f32[2,6,2,512]{3,2,1,0:T(2,128)} %get-tuple-element.69.refs_7_.refs_10_.refs_8_) | copy-start | bytes 147460
  222.4 31.0 %collective-permute-start.18 = (bf16[2,2,2,2,1,96,768]{6,5,4,3,2,1,0:T(8,128)(2,1)}, bf16[2,2,2,2,1,96,768]{6,5,4,3,2,1,0:T(8,128)(2,1)}, u32[]{:S(2)}, u32[]{:S(2)}) collective-permute-start(bf16[2,2,2,2,1,96,768]{6,5,4,3,2,1,0:T(8,128)(2,1)} %constant_dynamic-slice_fusion.11.refs_0_), channel_id=1, source_target_pairs={{0,1},{1,0},{2,3},{3,2},{4,5},{5,4},{6,7},{7,6},{8,9},{9,8},{10,11... | collective-permute-start | bytes 7077896 | tf_op jit(solution)/shard_map/ppermute | solution.py:475
  223.7 29.8 %slice-start = ((s8[4718592]{0:T(1024)(128)(4,1)}), s8[4194304]{0:T(1024)(128)(4,1)S(1)}, s32[]{:S(2)}) async-start(s8[4718592]{0:T(1024)(128)(4,1)} %bitcast.97), calls=%async_computation.3 | async-start | bytes 8388608
  224.5 17.5 %collective-permute-start.16 = (bf16[1,512,384]{2,1,0:T(8,128)(2,1)S(1)}, bf16[1,512,384]{2,1,0:T(8,128)(2,1)S(1)}, u32[]{:S(2)}, u32[]{:S(2)}) collective-permute-start(bf16[1,512,384]{2,1,0:T(8,128)(2,1)S(1)} %get-tuple-element.112), channel_id=1, source_target_pairs={{16,0},{17,1},{18,2},{19,3},{20,4},{21,5},{22,6},{23,7},{24,8},{25... | collective-permute-start | bytes 1179656 | tf_op jit(solution)/shard_map/ppermute | solution.py:741
  226.0 27.5 %slice-start.1 = ((s8[4718592]{0:T(1024)(128)(4,1)}), s8[524288]{0:T(1024)(128)(4,1)S(1)}, s32[]{:S(2)}) async-start(s8[4718592]{0:T(1024)(128)(4,1)} %bitcast.97), calls=%async_computation.4 | async-start | bytes 1048576
  226.0 16.0 %collective-permute-start.17 = (f32[2,2,3,2,512]{4,3,2,1,0:T(2,128)S(1)}, f32[2,2,3,2,512]{4,3,2,1,0:T(2,128)S(1)}, u32[]{:S(2)}, u32[]{:S(2)}) collective-permute-start(f32[2,2,3,2,512]{4,3,2,1,0:T(2,128)S(1)} %pad_maximum_fusion.9), channel_id=1, source_target_pairs={{16,0},{17,1},{18,2},{19,3},{20,4},{21,5},{22,6},{23,7},{24,8},{25... | collective-permute-start | bytes 147464 | tf_op jit(solution)/shard_map/ppermute | solution.py:743
  237.9 38.2 %collective-permute-start.21 = (bf16[1,512,384]{2,1,0:T(8,128)(2,1)}, bf16[1,512,384]{2,1,0:T(8,128)(2,1)}, u32[]{:S(2)}, u32[]{:S(2)}) collective-permute-start(bf16[1,512,384]{2,1,0:T(8,128)(2,1)} %get-tuple-element.111), channel_id=1, source_target_pairs={{16,0},{17,1},{18,2},{19,3},{20,4},{21,5},{22,6},{23,7},{24,8},{25... | collective-permute-start | bytes 1179656 | tf_op jit(solution)/shard_map/ppermute | solution.py:741
  249.9 47.7 %collective-permute-start.20 = (bf16[1,512,768]{2,1,0:T(8,128)(2,1)}, bf16[1,512,768]{2,1,0:T(8,128)(2,1)}, u32[]{:S(2)}, u32[]{:S(2)}) collective-permute-start(bf16[1,512,768]{2,1,0:T(8,128)(2,1)} %get-tuple-element.73.refs_0_.refs_6_.refs_9_), channel_id=1, source_target_pairs={{0,16},{16,0},{1,17},{17,1},{2,18},{18,2},{3,19},{19,3},{4,20},{20... | collective-permute-start | bytes 2359304 | tf_op jit(solution)/shard_map/ppermute | solution.py:779
  255.9 5.2 %copy-start.11 = (bf16[2,2,1,2,1,96,768]{6,5,4,3,2,1,0:T(8,128)(2,1)}, bf16[2,2,1,2,1,96,768]{6,5,4,3,2,1,0:T(8,128)(2,1)S(1)}, u32[]{:S(2)}) copy-start(bf16[2,2,1,2,1,96,768]{6,5,4,3,2,1,0:T(8,128)(2,1)S(1)} %constant_dynamic-slice_fusion.9.refs_1_) | copy-start | bytes 3538948
  255.9 38.7 %collective-permute-start.25 = (bf16[2,2,1,2,1,96,768]{6,5,4,3,2,1,0:T(8,128)(2,1)S(1)}, bf16[2,2,1,2,1,96,768]{6,5,4,3,2,1,0:T(8,128)(2,1)}, u32[]{:S(2)}, u32[]{:S(2)}) collective-permute-start(bf16[2,2,1,2,1,96,768]{6,5,4,3,2,1,0:T(8,128)(2,1)S(1)} %constant_dynamic-slice_fusion.9.refs_1_), channel_id=1, source_target_pairs={{0,4},{1,5},{2,6},{3,7},{4,0},{5,1},{6,2},{7,3},{8,12},{9,13},{10,... | collective-permute-start | bytes 3538952 | tf_op jit(solution)/shard_map/ppermute | solution.py:475
  264.0 50.4 %collective-permute-start.27 = (bf16[2,2,2,1,1,24,3840]{6,5,4,3,2,1,0:T(8,128)(2,1)}, bf16[2,2,2,1,1,24,3840]{6,5,4,3,2,1,0:T(8,128)(2,1)}, u32[]{:S(2)}, u32[]{:S(2)}) collective-permute-start(bf16[2,2,2,1,1,24,3840]{6,5,4,3,2,1,0:T(8,128)(2,1)} %constant_dynamic-slice_fusion.8.refs_2_), channel_id=1, source_target_pairs={{0,2},{1,3},{2,0},{3,1},{4,6},{5,7},{6,4},{7,5},{8,10},{9,11},{10,... | collective-permute-start | bytes 4423688 | tf_op jit(solution)/shard_map/ppermute | solution.py:475
  276.1 7.4 %copy-start.3 = (bf16[2,512,768]{2,1,0:T(8,128)(2,1)S(1)}, bf16[2,512,768]{2,1,0:T(8,128)(2,1)}, u32[]{:S(2)}) copy-start(bf16[2,512,768]{2,1,0:T(8,128)(2,1)} %param.15) | copy-start | bytes 4718596
  283.4 19.2 %collective-permute-start.22 = (bf16[1,512,768]{2,1,0:T(8,128)(2,1)}, bf16[1,512,768]{2,1,0:T(8,128)(2,1)}, u32[]{:S(2)}, u32[]{:S(2)}) collective-permute-start(bf16[1,512,768]{2,1,0:T(8,128)(2,1)} %get-tuple-element.78.refs_9_.refs_12_), channel_id=1, source_target_pairs={{0,16},{16,0},{1,17},{17,1},{2,18},{18,2},{3,19},{19,3},{4,20},{20... | collective-permute-start | bytes 2359304 | tf_op jit(solution)/shard_map/ppermute | solution.py:779
  296.2 6.4 %copy-start.13 = (bf16[2,2,1,2,1,96,768]{6,5,4,3,2,1,0:T(8,128)(2,1)}, bf16[2,2,1,2,1,96,768]{6,5,4,3,2,1,0:T(8,128)(2,1)S(1)}, u32[]{:S(2)}) copy-start(bf16[2,2,1,2,1,96,768]{6,5,4,3,2,1,0:T(8,128)(2,1)S(1)} %add_convert_fusion.5) | copy-start | bytes 3538948
  297.2 34.8 %collective-permute-start.26 = (bf16[2,2,1,1,1,96,768]{6,5,4,3,2,1,0:T(8,128)(2,1)}, bf16[2,2,1,1,1,96,768]{6,5,4,3,2,1,0:T(8,128)(2,1)}, u32[]{:S(2)}, u32[]{:S(2)}) collective-permute-start(bf16[2,2,1,1,1,96,768]{6,5,4,3,2,1,0:T(8,128)(2,1)} %constant_dynamic-slice_fusion.4), channel_id=1, source_target_pairs={{0,2},{1,3},{2,0},{3,1},{4,6},{5,7},{6,4},{7,5},{8,10},{9,11},{10,... | collective-permute-start | bytes 1769480 | tf_op jit(solution)/shard_map/ppermute | solution.py:475
  302.6 11.9 %copy-start.7 = (bf16[2,2,2,2,1,24,3840]{6,5,4,3,2,1,0:T(8,128)(2,1)S(1)}, bf16[2,2,2,2,1,24,3840]{6,5,4,3,2,1,0:T(8,128)(2,1)}, u32[]{:S(2)}) copy-start(bf16[2,2,2,2,1,24,3840]{6,5,4,3,2,1,0:T(8,128)(2,1)} %copy-done.6) | copy-start | bytes 8847364
  313.1 4.6 %collective-permute-start.23 = (bf16[2,2,2,2,1,24,1152]{6,5,4,3,2,1,0:T(8,128)(2,1)}, bf16[2,2,2,2,1,24,1152]{6,5,4,3,2,1,0:T(8,128)(2,1)}, u32[]{:S(2)}, u32[]{:S(2)}) collective-permute-start(bf16[2,2,2,2,1,24,1152]{6,5,4,3,2,1,0:T(8,128)(2,1)} %constant_dynamic-slice_fusion.7), channel_id=1, source_target_pairs={{0,1},{1,0},{2,3},{3,2},{4,5},{5,4},{6,7},{7,6},{8,9},{9,8},{10,11... | collective-permute-start | bytes 2654216 | tf_op jit(solution)/shard_map/ppermute | solution.py:475
  316.3 4.5 %copy-start.9 = (bf16[2,2,2,1,1,24,3840]{6,5,4,3,2,1,0:T(8,128)(2,1)}, bf16[2,2,2,1,1,24,3840]{6,5,4,3,2,1,0:T(8,128)(2,1)S(1)}, u32[]{:S(2)}) copy-start(bf16[2,2,2,1,1,24,3840]{6,5,4,3,2,1,0:T(8,128)(2,1)S(1)} %add_convert_fusion.4) | copy-start | bytes 4423684
  317.3 21.0 %collective-permute-start.28 = (bf16[1,2,2,1,1,24,3840]{6,5,4,3,2,1,0:T(8,128)(2,1)}, bf16[1,2,2,1,1,24,3840]{6,5,4,3,2,1,0:T(8,128)(2,1)}, u32[]{:S(2)}, u32[]{:S(2)}) collective-permute-start(bf16[1,2,2,1,1,24,3840]{6,5,4,3,2,1,0:T(8,128)(2,1)} %constant_dynamic-slice_fusion.3), channel_id=1, source_target_pairs={{0,16},{16,0},{1,17},{17,1},{2,18},{18,2},{3,19},{19,3},{4,20},{20... | collective-permute-start | bytes 2211848 | tf_op jit(solution)/shard_map/ppermute | solution.py:473
  320.8 36.0 %collective-permute-start.29 = (bf16[1,2,2,2,1,24,1152]{6,5,4,3,2,1,0:T(8,128)(2,1)}, bf16[1,2,2,2,1,24,1152]{6,5,4,3,2,1,0:T(8,128)(2,1)}, u32[]{:S(2)}, u32[]{:S(2)}) collective-permute-start(bf16[1,2,2,2,1,24,1152]{6,5,4,3,2,1,0:T(8,128)(2,1)} %constant_dynamic-slice_fusion.6.refs_0_), channel_id=1, source_target_pairs={{0,16},{16,0},{1,17},{17,1},{2,18},{18,2},{3,19},{19,3},{4,20},{20... | collective-permute-start | bytes 1327112 | tf_op jit(solution)/shard_map/ppermute | solution.py:473
  331.9 11.0 %collective-permute-start.24 = (bf16[2,2,2,2,1,24,1152]{6,5,4,3,2,1,0:T(8,128)(2,1)S(1)}, bf16[2,2,2,2,1,24,1152]{6,5,4,3,2,1,0:T(8,128)(2,1)}, u32[]{:S(2)}, u32[]{:S(2)}) collective-permute-start(bf16[2,2,2,2,1,24,1152]{6,5,4,3,2,1,0:T(8,128)(2,1)S(1)} %constant_dynamic-slice_fusion.5.refs_1_), channel_id=1, source_target_pairs={{0,1},{1,0},{2,3},{3,2},{4,5},{5,4},{6,7},{7,6},{8,9},{9,8},{10,11... | collective-permute-start | bytes 2654216 | tf_op jit(solution)/shard_map/ppermute | solution.py:475
  332.9 5.5 %copy-start.10 = (bf16[2,2,2,1,1,24,3840]{6,5,4,3,2,1,0:T(8,128)(2,1)S(1)}, bf16[2,2,2,1,1,24,3840]{6,5,4,3,2,1,0:T(8,128)(2,1)}, u32[]{:S(2)}) copy-start(bf16[2,2,2,1,1,24,3840]{6,5,4,3,2,1,0:T(8,128)(2,1)} %copy-done.9) | copy-start | bytes 4423684
  336.0 37.6 %collective-permute-start.31 = (bf16[2,1,1,1,1,96,768]{6,5,4,3,2,1,0:T(8,128)(2,1)}, bf16[2,1,1,1,1,96,768]{6,5,4,3,2,1,0:T(8,128)(2,1)}, u32[]{:S(2)}, u32[]{:S(2)}) collective-permute-start(bf16[2,1,1,1,1,96,768]{6,5,4,3,2,1,0:T(8,128)(2,1)} %dynamic-slice_convert_fusion.1.refs_1_), channel_id=1, source_target_pairs={{0,8},{1,9},{2,10},{3,11},{4,12},{5,13},{6,14},{7,15},{8,0},{9,1},... | collective-permute-start | bytes 884744 | tf_op jit(solution)/shard_map/ppermute | solution.py:475
  341.5 35.3 %collective-permute-start.33 = (bf16[1,2,1,1,1,24,3840]{6,5,4,3,2,1,0:T(8,128)(2,1)}, bf16[1,2,1,1,1,24,3840]{6,5,4,3,2,1,0:T(8,128)(2,1)}, u32[]{:S(2)}, u32[]{:S(2)}) collective-permute-start(bf16[1,2,1,1,1,24,3840]{6,5,4,3,2,1,0:T(8,128)(2,1)} %dynamic-slice_convert_fusion.refs_2_), channel_id=1, source_target_pairs={{0,4},{1,5},{2,6},{3,7},{4,0},{5,1},{6,2},{7,3},{8,12},{9,13},{10,... | collective-permute-start | bytes 1105928 | tf_op jit(solution)/shard_map/ppermute | solution.py:475
  345.2 25.9 %collective-permute-start.32 = (bf16[2,2,2,1,1,24,1152]{6,5,4,3,2,1,0:T(8,128)(2,1)}, bf16[2,2,2,1,1,24,1152]{6,5,4,3,2,1,0:T(8,128)(2,1)}, u32[]{:S(2)}, u32[]{:S(2)}) collective-permute-start(bf16[2,2,2,1,1,24,1152]{6,5,4,3,2,1,0:T(8,128)(2,1)} %constant_dynamic-slice_fusion.2.refs_0_), channel_id=1, source_target_pairs={{0,2},{1,3},{2,0},{3,1},{4,6},{5,7},{6,4},{7,5},{8,10},{9,11},{10,... | collective-permute-start | bytes 1327112 | tf_op jit(solution)/shard_map/ppermute | solution.py:475
  345.7 11.1 %copy-start.20 = (bf16[2,2,2,2,1,24,1152]{6,5,4,3,2,1,0:T(8,128)(2,1)S(1)}, bf16[2,2,2,2,1,24,1152]{6,5,4,3,2,1,0:T(8,128)(2,1)}, u32[]{:S(2)}) copy-start(bf16[2,2,2,2,1,24,1152]{6,5,4,3,2,1,0:T(8,128)(2,1)} %copy-done.19) | copy-start | bytes 2654212
  345.7 12.5 %copy-start.38 = (f32[32,24]{1,0:T(8,128)S(1)}, f32[32,24]{1,0:T(8,128)}, u32[]{:S(2)}) copy-start(f32[32,24]{1,0:T(8,128)} %reshape_squeeze.21) | copy-start | bytes 9220
  345.7 12.5 %copy-start.39 = (f32[32,24]{1,0:T(8,128)S(1)}, f32[32,24]{1,0:T(8,128)}, u32[]{:S(2)}) copy-start(f32[32,24]{1,0:T(8,128)} %reshape_squeeze.22) | copy-start | bytes 9220
  345.7 12.5 %copy-start.40 = (f32[32,24]{1,0:T(8,128)S(1)}, f32[32,24]{1,0:T(8,128)}, u32[]{:S(2)}) copy-start(f32[32,24]{1,0:T(8,128)} %reshape_squeeze.23) | copy-start | bytes 9220
  345.7 12.5 %copy-start.41 = (f32[32,96]{1,0:T(8,128)S(1)}, f32[32,96]{1,0:T(8,128)}, u32[]{:S(2)}) copy-start(f32[32,96]{1,0:T(8,128)} %reshape.202) | copy-start | bytes 36868
  345.7 12.5 %copy-start.42 = (f32[32,24]{1,0:T(8,128)S(1)}, f32[32,24]{1,0:T(8,128)}, u32[]{:S(2)}) copy-start(f32[32,24]{1,0:T(8,128)} %reshape.200) | copy-start | bytes 9220
  345.7 12.5 %copy-start.43 = (f32[32,24]{1,0:T(8,128)S(1)}, f32[32,24]{1,0:T(8,128)}, u32[]{:S(2)}) copy-start(f32[32,24]{1,0:T(8,128)} %reshape.201) | copy-start | bytes 9220
  358.0 13.1 %copy-start.22 = (bf16[1,2,2,2,1,24,1152]{6,5,4,3,2,1,0:T(8,128)(2,1)}, bf16[1,2,2,2,1,24,1152]{6,5,4,3,2,1,0:T(8,128)(2,1)S(1)}, u32[]{:S(2)}) copy-start(bf16[1,2,2,2,1,24,1152]{6,5,4,3,2,1,0:T(8,128)(2,1)S(1)} %add_convert_fusion.9) | copy-start | bytes 1327108
  358.0 15.7 %copy-start.18 = (f32[2,2,1,1,1,96,768]{6,5,4,3,2,1,0:T(8,128)S(1)}, f32[2,2,1,1,1,96,768]{6,5,4,3,2,1,0:T(8,128)}, u32[]{:S(2)}) copy-start(f32[2,2,1,1,1,96,768]{6,5,4,3,2,1,0:T(8,128)} %copy-done.17) | copy-start | bytes 3538948
  359.0 10.8 %all-to-all-start = ((f32[32,1,288]{2,1,0:T(1,128)}), f32[32,1,288]{2,1,0:T(1,128)S(1)}, u32[]{:S(2)}, u32[]{:S(2)}) async-start(f32[32,1,288]{2,1,0:T(1,128)} %all_to_all.6), calls=%async_computation | async-start | bytes 98304 | tf_op jit(solution)/shard_map/all_to_all | solution.py:813
  363.1 15.5 %collective-permute-start.30 = (bf16[1,2,2,1,1,24,1152]{6,5,4,3,2,1,0:T(8,128)(2,1)}, bf16[1,2,2,1,1,24,1152]{6,5,4,3,2,1,0:T(8,128)(2,1)}, u32[]{:S(2)}, u32[]{:S(2)}) collective-permute-start(bf16[1,2,2,1,1,24,1152]{6,5,4,3,2,1,0:T(8,128)(2,1)} %constant_dynamic-slice_fusion.1.refs_1_), channel_id=1, source_target_pairs={{0,2},{1,3},{2,0},{3,1},{4,6},{5,7},{6,4},{7,5},{8,10},{9,11},{10,... | collective-permute-start | bytes 663560 | tf_op jit(solution)/shard_map/ppermute | solution.py:475
  373.0 8.5 %collective-permute-start.34 = (bf16[1,2,2,1,1,24,1152]{6,5,4,3,2,1,0:T(8,128)(2,1)S(1)}, bf16[1,2,2,1,1,24,1152]{6,5,4,3,2,1,0:T(8,128)(2,1)}, u32[]{:S(2)}, u32[]{:S(2)}) collective-permute-start(bf16[1,2,2,1,1,24,1152]{6,5,4,3,2,1,0:T(8,128)(2,1)S(1)} %constant_dynamic-slice_fusion.refs_2_), channel_id=1, source_target_pairs={{0,16},{16,0},{1,17},{17,1},{2,18},{18,2},{3,19},{19,3},{4,20},{20... | collective-permute-start | bytes 663560 | tf_op jit(solution)/shard_map/ppermute | solution.py:473
  375.4 8.3 %collective-permute-start.38 = (bf16[1,1,1,1,1,96,768]{6,5,4,3,2,1,0:T(8,128)(2,1)}, bf16[1,1,1,1,1,96,768]{6,5,4,3,2,1,0:T(8,128)(2,1)}, u32[]{:S(2)}, u32[]{:S(2)}) collective-permute-start(bf16[1,1,1,1,1,96,768]{6,5,4,3,2,1,0:T(8,128)(2,1)} %dynamic-slice_convert_fusion.3.refs_1_), channel_id=1, source_target_pairs={{0,16},{16,0},{1,17},{17,1},{2,18},{18,2},{3,19},{19,3},{4,20},{20... | collective-permute-start | bytes 442376 | tf_op jit(solution)/shard_map/ppermute | solution.py:473
  378.0 14.2 %collective-permute-start.37 = (bf16[1,1,1,1,1,24,3840]{6,5,4,3,2,1,0:T(8,128)(2,1)S(1)}, bf16[1,1,1,1,1,24,3840]{6,5,4,3,2,1,0:T(8,128)(2,1)S(1)}, u32[]{:S(2)}, u32[]{:S(2)}) collective-permute-start(bf16[1,1,1,1,1,24,3840]{6,5,4,3,2,1,0:T(8,128)(2,1)S(1)} %dynamic-slice_convert_fusion.2.refs_2_), channel_id=1, source_target_pairs={{0,8},{1,9},{2,10},{3,11},{4,12},{5,13},{6,14},{7,15},{8,0},{9,1},... | collective-permute-start | bytes 552968 | tf_op jit(solution)/shard_map/ppermute | solution.py:475
  382.5 9.5 %collective-permute-start.35 = (bf16[1,2,1,1,1,24,2304]{6,5,4,3,2,1,0:T(8,128)(2,1)S(1)}, bf16[1,2,1,1,1,24,2304]{6,5,4,3,2,1,0:T(8,128)(2,1)S(1)}, u32[]{:S(2)}, u32[]{:S(2)}) collective-permute-start(bf16[1,2,1,1,1,24,2304]{6,5,4,3,2,1,0:T(8,128)(2,1)S(1)} %fusion.5), channel_id=1, source_target_pairs={{0,4},{1,5},{2,6},{3,7},{4,0},{5,1},{6,2},{7,3},{8,12},{9,13},{10,... | collective-permute-start | bytes 663560 | tf_op jit(solution)/shard_map/ppermute | solution.py:475
  392.1 5.9 %collective-permute-start.36 = (bf16[1,1,1,1,1,24,2304]{6,5,4,3,2,1,0:T(8,128)(2,1)S(1)}, bf16[1,1,1,1,1,24,2304]{6,5,4,3,2,1,0:T(8,128)(2,1)S(1)}, u32[]{:S(2)}, u32[]{:S(2)}) collective-permute-start(bf16[1,1,1,1,1,24,2304]{6,5,4,3,2,1,0:T(8,128)(2,1)S(1)} %dynamic-slice_convert_fusion.4), channel_id=1, source_target_pairs={{0,8},{1,9},{2,10},{3,11},{4,12},{5,13},{6,14},{7,15},{8,0},{9,1},... | collective-permute-start | bytes 331784 | tf_op jit(solution)/shard_map/ppermute | solution.py:475
  (28 other events, 49.2 us)
Sparse Core Ops, SparseCore 0:
  10.9 69.2 all-gather.4
  83.7 70.6 all-gather.2
where the time goes:
time: 411 us; the launch traced here: 406 us
  Pallas kernels  164 us (40%)
  waiting for transfers between devices  82.6 us (20%)
  local copies, waits for them, and re-layouts  57.5 us (14%)
  starting transfers between devices  48.9 us (12%)
  other arithmetic  31.6 us (8%)
  between operations  15.3 us (4%)
  matrix products  6.12 us (1%)
    pallas_call x1, Pallas kernels, middle_part(): call(middle_kernel, (steps + 1,), [act, act, once((width, width), steps),...  56.6 us
    ppermute x22, waiting for transfers between devices, swap(): lax.ppermute(value, 'fsdp', [(i, i ^ flip) for i in range(self.fsdp)])  28.9 us
    pallas_call x2, Pallas kernels, local_forward(): call(local_forward_kernel, (pairs,), [own(b, 0), own(b, 1), own(b, 2)], [...  21.1 us
    pallas_call x2, Pallas kernels, local_backward(): call(local_backward_kernel, (pairs,), [own(b, 0), own(b, 1), own(b, 2), c...  20.9 us
    ppermute x2, waiting for transfers between devices, per_device(): arrived.append(lax.ppermute(send, 'seq', both_ways))  19.4 us
    ppermute x22, starting transfers between devices, swap(): lax.ppermute(value, 'fsdp', [(i, i ^ flip) for i in range(self.fsdp)])  19.2 us
    pallas_call x2, Pallas kernels, join(): call(functools.partial(join_kernel, first), (count,), [SCALAR, pl.BlockSp...  16.4 us
    pallas_call x2, Pallas kernels, cross_forward(): call(cross_forward_kernel, (hp,), [SCALAR, own(b, 0), own(b, 1, 1), own(b...  15.5 us
  transfers between devices with their start and end apart: 42, of which 18 were waited for; matrix products, arithmetic and copies ran while one was open for 19% of the time, Pallas kernels for 26%

commit v1 on v0

--- a/solution.py
+++ b/solution.py
@@ -700,10 +700,9 @@
         arrived.append(lax.ppermute(send, "seq", both_ways))
     for b in range(seqs):
         local.append(local_forward(b, packed))
-    after = (local[-1][0],)
+    after = tuple(o1 for o1, _ in local)
     for b in range(seqs):
         o2, l2 = cross_forward(b, arrived[b], after)
-        after = (o2,)
         o3, l3 = lax.ppermute(o2, "seq", forth), lax.ppermute(l2, "seq", forth)
         cross.append((o2, l2, o3, l3))
     flat = [item for b in range(seqs) for item in local[b] + cross[b]]

time: 411 us -> 406 us (0.988)
  waiting for transfers between devices: 82.6 us -> 74.8 us
    ppermute x2, waiting for transfers between devices: 19.4 us -> 5.99 us  [per_device(): arrived.append(lax.ppermute(send, 'seq', both_ways))]
    all_gather x1, waiting for transfers between devices: 0.01 us -> 6.01 us  [per_device(): lax.all_gather(jnp.concatenate([w_up, w_proj], axis=1), ('seq', 'fsdp'),...]
    unnamed x110 -> x108, local copies, waits for them, and re-layouts: 12.8 us -> 12.8 us
  transfers between devices with their start and end apart: 42 -> 42, of which waited for: 18 -> 18; matrix products, arithmetic and copies ran while one was open for 19% -> 20% of each run, Pallas kernels for 26% -> 27%
where the time goes in v1:
time: 406 us; the launch traced here: 400 us
  Pallas kernels  164 us (40%)
  waiting for transfers between devices  74.8 us (18%)
  local copies, waits for them, and re-layouts  57.3 us (14%)
  starting transfers between devices  51.3 us (13%)
  other arithmetic  31.6 us (8%)
  between operations  15.2 us (4%)
  matrix products  6.12 us (2%)
    pallas_call x1, Pallas kernels, middle_part(): call(middle_kernel, (steps + 1,), [act, act, once((width, width), steps),...  56.6 us
    ppermute x22, waiting for transfers between devices, swap(): lax.ppermute(value, 'fsdp', [(i, i ^ flip) for i in range(self.fsdp)])  28.9 us
    pallas_call x2, Pallas kernels, local_forward(): call(local_forward_kernel, (pairs,), [own(b, 0), own(b, 1), own(b, 2)], [...  21.1 us
    pallas_call x2, Pallas kernels, local_backward(): call(local_backward_kernel, (pairs,), [own(b, 0), own(b, 1), own(b, 2), c...  20.9 us
    ppermute x22, starting transfers between devices, swap(): lax.ppermute(value, 'fsdp', [(i, i ^ flip) for i in range(self.fsdp)])  19.2 us
    pallas_call x2, Pallas kernels, join(): call(functools.partial(join_kernel, first), (count,), [SCALAR, pl.BlockSp...  16.3 us
    pallas_call x2, Pallas kernels, cross_forward(): call(cross_forward_kernel, (hp,), [SCALAR, own(b, 0), own(b, 1, 1), own(b...  15.4 us
    dynamic_slice x12, local copies, waits for them, and re-layouts, send(): sent = lax.dynamic_index_in_dim(self.value, 1 - own, dim, keepdims=True)  14.7 us
  transfers between devices with their start and end apart: 42, of which 18 were waited for; matrix products, arithmetic and copies ran while one was open for 20% of the time, Pallas kernels for 27%

profile of v1, /device:TPU:0, one launch (start us, length us, event | category | flops | bytes accessed | tf_op | source)
XLA Modules:
  0.0 400.1 jit_solution(1951766508765643578)
XLA Ops:
  8.0 1.6 pad_maximum_fusion.6
  9.6 6.1 %concatenate.58 = bf16[288]{0:T(512)(128)(2,1)S(1)} concatenate(bf16[24]{0:T(256)(128)(2,1)} %param.17, bf16[24]{0:T(256)(128)(2,1)} %param.18, bf16[24]{0:T(256)(128)(2,1)} %param.20, bf16[24]{0:T(256)(128)(2,1)} %param.21, bf16[24]{0:T(256)(128)(2,1)} %param.23, bf16[24]{0:T(256)(128)(2,1)} %param.24, bf16[24]{0:T(256)(128)(2,1)} %param.25, bf16[24]{0:T(256)(128)(2,1)} %param.29, ...), dimensions={0} | concatenate | bytes 1152 | tf_op jit(solution)/shard_map/concatenate | solution.py:610
  16.6 4.1 %collective-permute-start.5 = (bf16[1,24,1280]{2,1,0:T(8,128)(2,1)S(1)}, bf16[1,24,1280]{2,1,0:T(8,128)(2,1)S(1)}, u32[]{:S(2)}, u32[]{:S(2)}) collective-permute-start(bf16[1,24,1280]{2,1,0:T(8,128)(2,1)S(1)} %maximum_bitcast_fusion), channel_id=1, source_target_pairs={{0,8},{1,9},{2,10},{3,11},{4,12},{5,13},{6,14},{7,15},{8,0},{9,1},... | collective-permute-start | bytes 184328 | tf_op jit(solution)/shard_map/ppermute | solution.py:475
  21.6 4.6 %collective-permute-done = bf16[1,24,1152]{2,1,0:T(8,128)(2,1)S(1)} collective-permute-done((bf16[1,24,1152]{2,1,0:T(8,128)(2,1)S(1)}, bf16[1,24,1152]{2,1,0:T(8,128)(2,1)S(1)}, u32[]{:S(2)}, u32[]{:S(2)}) %collective-permute-start) | collective-permute-done | bytes 55328 | tf_op jit(solution)/shard_map/ppermute | solution.py:475
  26.2 2.1 collective-permute-start.1
  28.4 4.8 %collective-permute-done.1 = bf16[2,24,1152]{2,1,0:T(8,128)(2,1)S(1)} collective-permute-done((bf16[2,24,1152]{2,1,0:T(8,128)(2,1)S(1)}, bf16[2,24,1152]{2,1,0:T(8,128)(2,1)S(1)}, u32[]{:S(2)}, u32[]{:S(2)}) %collective-permute-start.1) | collective-permute-done | bytes 110624 | tf_op jit(solution)/shard_map/ppermute | solution.py:475
  33.3 2.4 collective-permute-start.2
  36.1 1.4 collective-permute-start.7
  37.6 8.9 %collective-permute-done.7 = bf16[4,24,1280]{2,1,0:T(8,128)(2,1)S(1)} collective-permute-done((bf16[4,24,1280]{2,1,0:T(8,128)(2,1)S(1)}, bf16[4,24,1280]{2,1,0:T(8,128)(2,1)S(1)}, u32[]{:S(2)}, u32[]{:S(2)}) %collective-permute-start.7) | collective-permute-done | bytes 245792 | tf_op jit(solution)/shard_map/ppermute | solution.py:473
  46.9 2.5 collective-permute-start.3
  49.5 6.5 %collective-permute-done.8 = bf16[8,24,1280]{2,1,0:T(8,128)(2,1)S(1)} collective-permute-done((bf16[8,24,1280]{2,1,0:T(8,128)(2,1)S(1)}, bf16[8,24,1280]{2,1,0:T(8,128)(2,1)S(1)}, u32[]{:S(2)}, u32[]{:S(2)}) %collective-permute-start.8) | collective-permute-done | bytes 491552 | tf_op jit(solution)/shard_map/ppermute | solution.py:475
  56.1 1.4 collective-permute-done.3
  58.6 1.6 collective-permute-done.4.refs_1_
  60.2 4.6 %place_qkv.1 = (bf16[32,24,2304]{2,1,0:T(8,128)(2,1)}, bf16[32,24,128]{2,1,0:T(8,128)(2,1)}) custom-call(s32[1]{0:T(128)} %bitcast.2.me, bf16[16,24,1152]{2,1,0:T(8,128)(2,1)} %copy-done.30, bf16[16,24,1152]{2,1,0:T(8,128)(2,1)} %collective-permute-done.4.refs_1_, bf16[16,24,1280]{2,1,0:T(8,128)(2,1)} %copy-done.29, ...), custom_call_target="tpu_custom_call" | custom-call | bytes 7471104 | tf_op jit(solution)/shard_map/place_qkv/pallas_call | solution.py:521
  67.1 6.1 %add_convert_fusion = bf16[1024,2304]{1,0:T(8,128)(2,1)S(1)} fusion(bf16[1024,768]{1,0:T(8,128)(2,1)S(1)} %bitcast.104, bf16[768,2304]{1,0:T(8,128)(2,1)} %bitcast.112, f32[2304]{0:T(1024)S(1)} %pad_maximum_fusion.10), kind=kOutput, calls=%fused_computation | convolution fusion | flops 3628597248 | bytes 9839616 | tf_op jit(solution)/shard_map/dot_general | solution.py:23
  73.6 1.8 copy-done
  75.5 1.7 collective-permute-start.13
  77.9 10.6 %local_forward_0.1 = (bf16[1,512,768]{2,1,0:T(8,128)(2,1)}, f32[1,6,2,512]{3,2,1,0:T(2,128)}) custom-call(bf16[2,512,2304]{2,1,0:T(8,128)(2,1)} %bitcast.63, bf16[2,512,2304]{2,1,0:T(8,128)(2,1)} %bitcast.64, bf16[2,512,2304]{2,1,0:T(8,128)(2,1)} %bitcast.65), custom_call_target="tpu_custom_call" | custom-call | flops 805306368 | bytes 3145728 | tf_op jit(solution)/shard_map/local_forward_0/pallas_call | solution.py:668
  88.4 10.6 %local_forward_1.1 = (bf16[1,512,768]{2,1,0:T(8,128)(2,1)}, f32[1,6,2,512]{3,2,1,0:T(2,128)}) custom-call(bf16[2,512,2304]{2,1,0:T(8,128)(2,1)} %bitcast.66, bf16[2,512,2304]{2,1,0:T(8,128)(2,1)} %bitcast.67, bf16[2,512,2304]{2,1,0:T(8,128)(2,1)} %bitcast.68), custom_call_target="tpu_custom_call" | custom-call | flops 805306368 | bytes 3145728 | tf_op jit(solution)/shard_map/local_forward_1/pallas_call | solution.py:668
  99.9 7.7 %cross_forward_1.1 = (bf16[1,512,384]{2,1,0:T(8,128)(2,1)}, f32[1,3,2,512]{3,2,1,0:T(2,128)}) custom-call(bf16[1,512,768]{2,1,0:T(8,128)(2,1)} %get-tuple-element.55.refs_0_, bf16[1,512,768]{2,1,0:T(8,128)(2,1)} %get-tuple-element.57.refs_1_.refs_6_, s32[1]{0:T(128)} %bitcast.1.refs_2_.late.refs_1_, bf16[2,512,2304]{2,1,0:T(8,128)(2,1)} %bitcast.69, ...), custom_call_target="tpu_custom_call" | custom-call | flops 402653184 | bytes 1572864 | tf_op jit(solution)/shard_map/cross_forward_1/pallas_call | solution.py:679
  107.6 3.7 collective-permute-start.14
  111.3 6.0 %collective-permute-done.10.refs_6_.refs_7_.refs_5_ = bf16[1,512,768]{2,1,0:T(8,128)(2,1)S(1)} collective-permute-done((bf16[1,512,768]{2,1,0:T(8,128)(2,1)S(1)}, bf16[1,512,768]{2,1,0:T(8,128)(2,1)S(1)}, u32[]{:S(2)}, u32[]{:S(2)}) %collective-permute-start.10) | collective-permute-done | bytes 786464 | tf_op jit(solution)/shard_map/ppermute | solution.py:700
  118.2 7.7 %cross_forward_0.1 = (bf16[1,512,384]{2,1,0:T(8,128)(2,1)}, f32[1,3,2,512]{3,2,1,0:T(2,128)}) custom-call(bf16[1,512,768]{2,1,0:T(8,128)(2,1)} %get-tuple-element.55.refs_0_, bf16[1,512,768]{2,1,0:T(8,128)(2,1)} %get-tuple-element.57.refs_1_.refs_6_, s32[1]{0:T(128)} %bitcast.1.refs_2_.late.refs_1_, bf16[2,512,2304]{2,1,0:T(8,128)(2,1)} %bitcast.74, ...), custom_call_target="tpu_custom_call" | custom-call | flops 402653184 | bytes 1572864 | tf_op jit(solution)/shard_map/cross_forward_0/pallas_call | solution.py:679
  125.9 4.4 %collective-permute-start.11 = (bf16[1,512,384]{2,1,0:T(8,128)(2,1)}, bf16[1,512,384]{2,1,0:T(8,128)(2,1)S(1)}, u32[]{:S(2)}, u32[]{:S(2)}) collective-permute-start(bf16[1,512,384]{2,1,0:T(8,128)(2,1)} %get-tuple-element.58.refs_2_), channel_id=1, source_target_pairs={{0,16},{1,17},{2,18},{3,19},{4,20},{5,21},{6,22},{7,23},{8,24},{9,... | collective-permute-start | bytes 1179656 | tf_op jit(solution)/shard_map/ppermute | solution.py:706
  136.3 7.4 %collective-permute-done.15.refs_11_ = f32[1,3,2,512]{3,2,1,0:T(2,128)S(1)} collective-permute-done((f32[1,3,2,512]{3,2,1,0:T(2,128)S(1)}, f32[1,3,2,512]{3,2,1,0:T(2,128)S(1)}, u32[]{:S(2)}, u32[]{:S(2)}) %collective-permute-start.15) | collective-permute-done | bytes 12320 | tf_op jit(solution)/shard_map/ppermute | solution.py:706
  145.1 4.1 %merge.1 = (bf16[2,512,768]{2,1,0:T(8,128)(2,1)}, f32[2,6,2,512]{3,2,1,0:T(2,128)}) custom-call(s32[1]{0:T(128)} %bitcast.1.refs_2_.late.refs_1_, bf16[1,512,768]{2,1,0:T(8,128)(2,1)} %get-tuple-element.55.refs_0_, f32[1,6,2,512]{3,2,1,0:T(2,128)} %get-tuple-element.56.refs_1_, bf16[1,512,384]{2,1,0:T(8,128)(2,1)} %get-tuple-element.58.refs_2_, ...), custom_call_target="tpu_custom_call" | custom-call | tf_op jit(solution)/shard_map/merge/pallas_call | solution.py:709
  149.1 6.0 %all-gather.3.cloned.1.call-done.w_proj.w_up = bf16[768,3840]{1,0:T(8,128)(2,1)} async-done(((bf16[24,3840]{1,0:T(8,128)(2,1)}), bf16[768,3840]{1,0:T(8,128)(2,1)}) %all-gather.3.cloned.1.call-update) | async-done | bytes 5898256 | tf_op jit(solution)/shard_map/all_gather | solution.py:618
  155.2 56.6 %middle_part.1 = (bf16[1024,768]{1,0:T(8,128)(2,1)}, f32[1024,768]{1,0:T(8,128)}, bf16[1024,768]{1,0:T(8,128)(2,1)}, f32[2,6,2,512]{3,2,1,0:T(2,128)}, f32[8,768...) custom-call(bf16[1024,768]{1,0:T(8,128)(2,1)} %bitcast.92, ...), custom_call_target="tpu_custom_call" | custom-call | flops 28991029248 | bytes 113246208 | tf_op jit(solution)/shard_map/middle_part/pallas_call | solution.py:306
  211.8 3.8 constant_dynamic-slice_fusion.10.refs_1_
  215.8 1.6 constant_dynamic-slice_fusion.11.refs_0_
  219.3 1.4 collective-permute-start.16
  220.8 1.4 collective-permute-start.17
  222.2 10.4 %local_backward_0.1 = (bf16[1,512,768]{2,1,0:T(8,128)(2,1)}, bf16[1,512,768]{2,1,0:T(8,128)(2,1)}, bf16[1,512,768]{2,1,0:T(8,128)(2,1)}) custom-call(bf16[2,2,2,2,1,96,768]{6,5,4,3,2,1,0:T(8,128)(2,1)} %constant_dynamic-slice_fusion.11.refs_0_, bf16[2,2,2,2,1,24,3840]{6,5,4,3,2,1,0:T(8,128)(2,1)} %constant_dynamic-slice_fusion.10.refs_1_, ...), custom_call_target="tpu_custom_call" | custom-call | flops 2415919104 | bytes 9437184 | tf_op jit(solution)/shard_map/local_backward_0/pallas_call | solution.py:746
  233.9 2.5 collective-permute-done.17.refs_11_.refs_12_
  237.3 7.2 %cross_backward_0.1 = (bf16[1,512,768]{2,1,0:T(8,128)(2,1)}, bf16[1,512,384]{2,1,0:T(8,128)(2,1)}) custom-call(bf16[1,512,768]{2,1,0:T(8,128)(2,1)} %get-tuple-element.70.refs_0_.refs_3_, s32[1]{0:T(128)} %bitcast.1.refs_2_.late.refs_1_, bf16[2,512,2304]{2,1,0:T(8,128)(2,1)} %bitcast.78, bf16[2,512,2304]{2,1,0:T(8,128)(2,1)} %bitcast.79, ...), custom_call_target="tpu_custom_call" | custom-call | flops 1207959552 | bytes 4718592 | tf_op jit(solution)/shard_map/cross_backward_0/pallas_call | solution.py:758
  244.4 3.5 collective-permute-start.20
  248.0 2.4 add_convert_fusion.2
  250.4 1.7 collective-permute-start.25
  252.2 3.4 add_convert_fusion.1
  255.6 1.6 copy-done.6
  258.5 1.6 collective-permute-start.27
  260.1 10.5 %local_backward_1.1 = (bf16[1,512,768]{2,1,0:T(8,128)(2,1)}, bf16[1,512,768]{2,1,0:T(8,128)(2,1)}, bf16[1,512,768]{2,1,0:T(8,128)(2,1)}) custom-call(bf16[1,512,768]{2,1,0:T(8,128)(2,1)} %get-tuple-element.73.refs_0_.refs_6_.refs_9_, bf16[2,2,1,2,1,96,768]{6,5,4,3,2,1,0:T(8,128)(2,1)} %copy-done.11, ...), custom_call_target="tpu_custom_call" | custom-call | flops 2415919104 | bytes 9437184 | tf_op jit(solution)/shard_map/local_backward_1/pallas_call | solution.py:746
  270.5 7.3 %cross_backward_1.1 = (bf16[1,512,768]{2,1,0:T(8,128)(2,1)}, bf16[1,512,384]{2,1,0:T(8,128)(2,1)}) custom-call(bf16[1,512,768]{2,1,0:T(8,128)(2,1)} %get-tuple-element.74.refs_0_.refs_3_.refs_6_, s32[1]{0:T(128)} %bitcast.1.refs_2_.late.refs_1_, bf16[2,512,2304]{2,1,0:T(8,128)(2,1)} %bitcast.84, bf16[2,512,2304]{2,1,0:T(8,128)(2,1)} %bitcast.85, ...), custom_call_target="tpu_custom_call" | custom-call | flops 1207959552 | bytes 4718592 | tf_op jit(solution)/shard_map/cross_backward_1/pallas_call | solution.py:758
  277.9 1.8 fusion.3.a1.refs_2_
  285.8 2.0 reduce.56
  287.8 1.4 reshape.202
  289.1 1.6 add_convert_fusion.5
  292.1 4.9 %collective-permute-done.22.refs_11_.refs_14_ = bf16[1,512,768]{2,1,0:T(8,128)(2,1)} collective-permute-done((bf16[1,512,768]{2,1,0:T(8,128)(2,1)}, bf16[1,512,768]{2,1,0:T(8,128)(2,1)}, u32[]{:S(2)}, u32[]{:S(2)}) %collective-permute-start.22) | collective-permute-done | bytes 786464 | tf_op jit(solution)/shard_map/ppermute | solution.py:778
  297.0 8.2 %join_0.1 = (bf16[1024,1152]{1,0:T(8,128)(2,1)}, bf16[768,1152]{1,0:T(8,128)(2,1)}, f32[1,1152]{1,0:T(1,128)}) custom-call(s32[1]{0:T(128)} %bitcast.1.refs_2_.late.refs_1_, bf16[1024,768]{1,0:T(8,128)(2,1)} %fusion.3.a1.refs_2_, bf16[1,512,768]{2,1,0:T(8,128)(2,1)} %get-tuple-element.70.refs_0_.refs_3_, ...), custom_call_target="tpu_custom_call" | custom-call | flops 1811939328 | bytes 7077888 | tf_op jit(solution)/shard_map/join_0/pallas_call | solution.py:382
  305.3 2.2 constant_dynamic-slice_fusion.7
  308.9 1.8 add_convert_fusion.4
  312.1 1.4 add_convert_fusion.7
  315.2 1.7 collective-permute-start.29
  316.9 8.1 %join_3.1 = (bf16[1024,1152]{1,0:T(8,128)(2,1)}, bf16[768,1152]{1,0:T(8,128)(2,1)}, f32[1,1152]{1,0:T(1,128)}) custom-call(bf16[1,2,2,2,1,24,1152]{6,5,4,3,2,1,0:T(8,128)(2,1)} %constant_dynamic-slice_fusion.6.refs_0_, s32[1]{0:T(128)} %bitcast.1.refs_2_.late.refs_1_, bf16[1024,768]{1,0:T(8,128)(2,1)} %fusion.3.a1.refs_2_, ...), custom_call_target="tpu_custom_call" | custom-call | flops 1811939328 | bytes 7077888 | tf_op jit(solution)/shard_map/join_3/pallas_call | solution.py:382
  337.3 1.4 add_convert_fusion.6
  340.1 10.2 %input_part.1 = (f32[1024,768]{1,0:T(8,128)}, f32[8,768]{1,0:T(8,128)}) custom-call(bf16[2,2,2,1,1,24,1152]{6,5,4,3,2,1,0:T(8,128)(2,1)} %constant_dynamic-slice_fusion.2.refs_0_, bf16[2,1,1,1,1,96,768]{6,5,4,3,2,1,0:T(8,128)(2,1)} %dynamic-slice_convert_fusion.1.refs_1_, bf16[1,2,1,1,1,24,3840]{6,5,4,3,2,1,0:T(8,128)(2,1)} %dynamic-slice_convert_fusion.refs_2_, ...), custom_call_target="tpu_custom_call" | custom-call | flops 3623878656 | bytes 14155776 | tf_op jit(solution)/shard_map/input_part/pallas_call | solution.py:423
  353.4 3.4 all-to-all-start
  357.5 1.8 collective-permute-start.30
  359.2 5.0 %all-to-all-done = f32[32,1,288]{2,1,0:T(1,128)S(1)} async-done(((f32[32,1,288]{2,1,0:T(1,128)}), f32[32,1,288]{2,1,0:T(1,128)S(1)}, u32[]{:S(2)}, u32[]{:S(2)}) %all-to-all-start) | async-done | bytes 36896 | tf_op jit(solution)/shard_map/all_to_all | solution.py:812
  369.8 1.4 collective-permute-start.38
  374.0 1.8 collective-permute-done.34.refs_0_
  378.1 1.7 add_bitcast_fusion.1
  379.7 6.6 %collective-permute-done.35 = bf16[1,2,1,1,1,24,2304]{6,5,4,3,2,1,0:T(8,128)(2,1)S(1)} collective-permute-done((bf16[1,2,1,1,1,24,2304]{6,5,4,3,2,1,0:T(8,128)(2,1)S(1)}, bf16[1,2,1,1,1,24,2304]{6,5,4,3,2,1,0:T(8,128)(2,1)S(1)}, u32[]{:S(2)}, u32[]{:S(2)}) %collective-permute-start.35) | collective-permute-done | bytes 221216 | tf_op jit(solution)/shard_map/ppermute | solution.py:475
  387.9 4.4 %collective-permute-done.36 = bf16[1,1,1,1,1,24,2304]{6,5,4,3,2,1,0:T(8,128)(2,1)S(1)} collective-permute-done((bf16[1,1,1,1,1,24,2304]{6,5,4,3,2,1,0:T(8,128)(2,1)S(1)}, bf16[1,1,1,1,1,24,2304]{6,5,4,3,2,1,0:T(8,128)(2,1)S(1)}, u32[]{:S(2)}, u32[]{:S(2)}) %collective-permute-start.36) | collective-permute-done | bytes 110624 | tf_op jit(solution)/shard_map/ppermute | solution.py:475
  (259 shorter events, 64.9 us)
Async XLA Ops:
  7.2 142.0 %all-gather.5.cloned.1.call-start = ((), (), s32[]{:S(2)}) async-start(), calls=%async_computation.2 | async-start | bytes 4866048 | tf_op jit(solution)/shard_map/all_gather | solution.py:621
  7.9 147.2 %all-gather.3.cloned.1.call-start = ((), (), s32[]{:S(2)}) async-start(), calls=%async_computation.1 | async-start | bytes 6082560 | tf_op jit(solution)/shard_map/all_gather | solution.py:618
  16.6 11.7 %collective-permute-start.5 = (bf16[1,24,1280]{2,1,0:T(8,128)(2,1)S(1)}, bf16[1,24,1280]{2,1,0:T(8,128)(2,1)S(1)}, u32[]{:S(2)}, u32[]{:S(2)}) collective-permute-start(bf16[1,24,1280]{2,1,0:T(8,128)(2,1)S(1)} %maximum_bitcast_fusion), channel_id=1, source_target_pairs={{0,8},{1,9},{2,10},{3,11},{4,12},{5,13},{6,14},{7,15},{8,0},{9,1},... | collective-permute-start | bytes 184328 | tf_op jit(solution)/shard_map/ppermute | solution.py:475
  20.7 5.5 %collective-permute-start = (bf16[1,24,1152]{2,1,0:T(8,128)(2,1)S(1)}, bf16[1,24,1152]{2,1,0:T(8,128)(2,1)S(1)}, u32[]{:S(2)}, u32[]{:S(2)}) collective-permute-start(bf16[1,24,1152]{2,1,0:T(8,128)(2,1)S(1)} %get-tuple-element.115), channel_id=1, source_target_pairs={{0,8},{1,9},{2,10},{3,11},{4,12},{5,13},{6,14},{7,15},{8,0},{9,1},... | collective-permute-start | bytes 165896 | tf_op jit(solution)/shard_map/ppermute | solution.py:475
  26.2 7.1 %collective-permute-start.1 = (bf16[2,24,1152]{2,1,0:T(8,128)(2,1)S(1)}, bf16[2,24,1152]{2,1,0:T(8,128)(2,1)S(1)}, u32[]{:S(2)}, u32[]{:S(2)}) collective-permute-start(bf16[2,24,1152]{2,1,0:T(8,128)(2,1)S(1)} %pad_maximum_fusion.8), channel_id=1, source_target_pairs={{0,4},{1,5},{2,6},{3,7},{4,0},{5,1},{6,2},{7,3},{8,12},{9,13},{10,... | collective-permute-start | bytes 331784 | tf_op jit(solution)/shard_map/ppermute | solution.py:475
  28.3 7.7 %collective-permute-start.6 = (bf16[2,24,1280]{2,1,0:T(8,128)(2,1)S(1)}, bf16[2,24,1280]{2,1,0:T(8,128)(2,1)S(1)}, u32[]{:S(2)}, u32[]{:S(2)}) collective-permute-start(bf16[2,24,1280]{2,1,0:T(8,128)(2,1)S(1)} %pad_maximum_fusion.7), channel_id=1, source_target_pairs={{0,4},{1,5},{2,6},{3,7},{4,0},{5,1},{6,2},{7,3},{8,12},{9,13},{10,... | collective-permute-start | bytes 368648 | tf_op jit(solution)/shard_map/ppermute | solution.py:475
  33.3 13.5 %collective-permute-start.2 = (bf16[4,24,1152]{2,1,0:T(8,128)(2,1)S(1)}, bf16[4,24,1152]{2,1,0:T(8,128)(2,1)S(1)}, u32[]{:S(2)}, u32[]{:S(2)}) collective-permute-start(bf16[4,24,1152]{2,1,0:T(8,128)(2,1)S(1)} %pad_maximum_fusion.5), channel_id=1, source_target_pairs={{0,2},{1,3},{2,0},{3,1},{4,6},{5,7},{6,4},{7,5},{8,10},{9,11},{10,... | collective-permute-start | bytes 663560 | tf_op jit(solution)/shard_map/ppermute | solution.py:475
  36.1 10.3 %collective-permute-start.7 = (bf16[4,24,1280]{2,1,0:T(8,128)(2,1)S(1)}, bf16[4,24,1280]{2,1,0:T(8,128)(2,1)S(1)}, u32[]{:S(2)}, u32[]{:S(2)}) collective-permute-start(bf16[4,24,1280]{2,1,0:T(8,128)(2,1)S(1)} %pad_maximum_fusion.4), channel_id=1, source_target_pairs={{0,16},{16,0},{1,17},{17,1},{2,18},{18,2},{3,19},{19,3},{4,20},{20... | collective-permute-start | bytes 737288 | tf_op jit(solution)/shard_map/ppermute | solution.py:473
  37.6 20.1 %copy-start.2 = (bf16[2,512,768]{2,1,0:T(8,128)(2,1)S(1)}, bf16[2,512,768]{2,1,0:T(8,128)(2,1)}, u32[]{:S(2)}) copy-start(bf16[2,512,768]{2,1,0:T(8,128)(2,1)} %param.15) | copy-start | bytes 4718596
  46.5 9.5 %collective-permute-start.8 = (bf16[8,24,1280]{2,1,0:T(8,128)(2,1)S(1)}, bf16[8,24,1280]{2,1,0:T(8,128)(2,1)S(1)}, u32[]{:S(2)}, u32[]{:S(2)}) collective-permute-start(bf16[8,24,1280]{2,1,0:T(8,128)(2,1)S(1)} %pad_maximum_fusion.2), channel_id=1, source_target_pairs={{0,2},{1,3},{2,0},{3,1},{4,6},{5,7},{6,4},{7,5},{8,10},{9,11},{10,... | collective-permute-start | bytes 1474568 | tf_op jit(solution)/shard_map/ppermute | solution.py:475
  46.9 10.6 %collective-permute-start.3 = (bf16[8,24,1152]{2,1,0:T(8,128)(2,1)S(1)}, bf16[8,24,1152]{2,1,0:T(8,128)(2,1)S(1)}, u32[]{:S(2)}, u32[]{:S(2)}) collective-permute-start(bf16[8,24,1152]{2,1,0:T(8,128)(2,1)S(1)} %pad_maximum_fusion.3), channel_id=1, source_target_pairs={{0,16},{16,0},{1,17},{17,1},{2,18},{18,2},{3,19},{19,3},{4,20},{20... | collective-permute-start | bytes 1327112 | tf_op jit(solution)/shard_map/ppermute | solution.py:473
  56.0 4.2 %copy-start.29 = (bf16[16,24,1280]{2,1,0:T(8,128)(2,1)}, bf16[16,24,1280]{2,1,0:T(8,128)(2,1)S(1)}, u32[]{:S(2)}) copy-start(bf16[16,24,1280]{2,1,0:T(8,128)(2,1)S(1)} %constant_dynamic-update-slice_fusion.5.refs_2_) | copy-start | bytes 2949124
  56.0 4.2 %collective-permute-start.9 = (bf16[16,24,1280]{2,1,0:T(8,128)(2,1)S(1)}, bf16[16,24,1280]{2,1,0:T(8,128)(2,1)}, u32[]{:S(2)}, u32[]{:S(2)}) collective-permute-start(bf16[16,24,1280]{2,1,0:T(8,128)(2,1)S(1)} %constant_dynamic-update-slice_fusion.5.refs_2_), channel_id=1, source_target_pairs={{0,1},{1,0},{2,3},{3,2},{4,5},{5,4},{6,7},{7,6},{8,9},{9,8},{10,11... | collective-permute-start | bytes 2949128 | tf_op jit(solution)/shard_map/ppermute | solution.py:475
  57.6 2.6 collective-permute-start.4
  75.5 23.5 %collective-permute-start.13 = (bf16[1,512,768]{2,1,0:T(8,128)(2,1)S(1)}, bf16[1,512,768]{2,1,0:T(8,128)(2,1)S(1)}, u32[]{:S(2)}, u32[]{:S(2)}) collective-permute-start(bf16[1,512,768]{2,1,0:T(8,128)(2,1)S(1)} %pad_maximum_fusion.1), channel_id=1, source_target_pairs={{0,16},{16,0},{1,17},{17,1},{2,18},{18,2},{3,19},{19,3},{4,20},{20... | collective-permute-start | bytes 2359304 | tf_op jit(solution)/shard_map/ppermute | solution.py:700
  77.4 39.9 %collective-permute-start.10 = (bf16[1,512,768]{2,1,0:T(8,128)(2,1)S(1)}, bf16[1,512,768]{2,1,0:T(8,128)(2,1)S(1)}, u32[]{:S(2)}, u32[]{:S(2)}) collective-permute-start(bf16[1,512,768]{2,1,0:T(8,128)(2,1)S(1)} %pad_maximum_fusion), channel_id=1, source_target_pairs={{0,16},{16,0},{1,17},{17,1},{2,18},{18,2},{3,19},{19,3},{4,20},{20... | collective-permute-start | bytes 2359304 | tf_op jit(solution)/shard_map/ppermute | solution.py:700
  107.6 22.7 %copy-start.43 = (f32[1,3,2,512]{3,2,1,0:T(2,128)S(1)}, f32[1,3,2,512]{3,2,1,0:T(2,128)}, u32[]{:S(2)}) copy-start(f32[1,3,2,512]{3,2,1,0:T(2,128)} %get-tuple-element.62.refs_9_) | copy-start | bytes 36868
  107.6 36.5 %collective-permute-start.14 = (bf16[1,512,384]{2,1,0:T(8,128)(2,1)}, bf16[1,512,384]{2,1,0:T(8,128)(2,1)S(1)}, u32[]{:S(2)}, u32[]{:S(2)}) collective-permute-start(bf16[1,512,384]{2,1,0:T(8,128)(2,1)} %get-tuple-element.61.refs_8_), channel_id=1, source_target_pairs={{0,16},{1,17},{2,18},{3,19},{4,20},{5,21},{6,22},{7,23},{8,24},{9,... | collective-permute-start | bytes 1179656 | tf_op jit(solution)/shard_map/ppermute | solution.py:706
  125.9 18.3 %collective-permute-start.11 = (bf16[1,512,384]{2,1,0:T(8,128)(2,1)}, bf16[1,512,384]{2,1,0:T(8,128)(2,1)S(1)}, u32[]{:S(2)}, u32[]{:S(2)}) collective-permute-start(bf16[1,512,384]{2,1,0:T(8,128)(2,1)} %get-tuple-element.58.refs_2_), channel_id=1, source_target_pairs={{0,16},{1,17},{2,18},{3,19},{4,20},{5,21},{6,22},{7,23},{8,24},{9,... | collective-permute-start | bytes 1179656 | tf_op jit(solution)/shard_map/ppermute | solution.py:706
  130.3 13.5 %collective-permute-start.15 = (f32[1,3,2,512]{3,2,1,0:T(2,128)S(1)}, f32[1,3,2,512]{3,2,1,0:T(2,128)S(1)}, u32[]{:S(2)}, u32[]{:S(2)}) collective-permute-start(f32[1,3,2,512]{3,2,1,0:T(2,128)S(1)} %copy-done.43), channel_id=1, source_target_pairs={{0,16},{1,17},{2,18},{3,19},{4,20},{5,21},{6,22},{7,23},{8,24},{9,... | collective-permute-start | bytes 36872 | tf_op jit(solution)/shard_map/ppermute | solution.py:706
  131.6 12.6 %collective-permute-start.12 = (f32[1,3,2,512]{3,2,1,0:T(2,128)}, f32[1,3,2,512]{3,2,1,0:T(2,128)S(1)}, u32[]{:S(2)}, u32[]{:S(2)}) collective-permute-start(f32[1,3,2,512]{3,2,1,0:T(2,128)} %get-tuple-element.59.refs_3_), channel_id=1, source_target_pairs={{0,16},{1,17},{2,18},{3,19},{4,20},{5,21},{6,22},{7,23},{8,24},{9,... | collective-permute-start | bytes 36872 | tf_op jit(solution)/shard_map/ppermute | solution.py:706
  211.7 4.1 %copy-start.12 = (bf16[3072,768]{1,0:T(8,128)(2,1)S(1)}, bf16[3072,768]{1,0:T(8,128)(2,1)}, u32[]{:S(2)}) copy-start(bf16[3072,768]{1,0:T(8,128)(2,1)} %get-tuple-element.65) | copy-start | bytes 14155780
  215.5 36.7 %collective-permute-start.19 = (bf16[2,2,2,2,1,24,3840]{6,5,4,3,2,1,0:T(8,128)(2,1)}, bf16[2,2,2,2,1,24,3840]{6,5,4,3,2,1,0:T(8,128)(2,1)}, u32[]{:S(2)}, u32[]{:S(2)}) collective-permute-start(bf16[2,2,2,2,1,24,3840]{6,5,4,3,2,1,0:T(8,128)(2,1)} %constant_dynamic-slice_fusion.10.refs_1_), channel_id=1, source_target_pairs={{0,1},{1,0},{2,3},{3,2},{4,5},{5,4},{6,7},{7,6},{8,9},{9,8},{10,11... | collective-permute-start | bytes 8847368 | tf_op jit(solution)/shard_map/ppermute | solution.py:475
  215.8 4.9 %copy-start.32 = (f32[2,6,2,512]{3,2,1,0:T(2,128)S(1)}, f32[2,6,2,512]{3,2,1,0:T(2,128)}, u32[]{:S(2)}) copy-start(f32[2,6,2,512]{3,2,1,0:T(2,128)} %get-tuple-element.69.refs_7_.refs_10_.refs_8_) | copy-start | bytes 147460
  217.4 30.5 %collective-permute-start.18 = (bf16[2,2,2,2,1,96,768]{6,5,4,3,2,1,0:T(8,128)(2,1)}, bf16[2,2,2,2,1,96,768]{6,5,4,3,2,1,0:T(8,128)(2,1)}, u32[]{:S(2)}, u32[]{:S(2)}) collective-permute-start(bf16[2,2,2,2,1,96,768]{6,5,4,3,2,1,0:T(8,128)(2,1)} %constant_dynamic-slice_fusion.11.refs_0_), channel_id=1, source_target_pairs={{0,1},{1,0},{2,3},{3,2},{4,5},{5,4},{6,7},{7,6},{8,9},{9,8},{10,11... | collective-permute-start | bytes 7077896 | tf_op jit(solution)/shard_map/ppermute | solution.py:475
  218.4 29.5 %slice-start = ((s8[4718592]{0:T(1024)(128)(4,1)}), s8[4194304]{0:T(1024)(128)(4,1)S(1)}, s32[]{:S(2)}) async-start(s8[4718592]{0:T(1024)(128)(4,1)} %bitcast.97), calls=%async_computation.3 | async-start | bytes 8388608
  219.3 17.2 %collective-permute-start.16 = (bf16[1,512,384]{2,1,0:T(8,128)(2,1)S(1)}, bf16[1,512,384]{2,1,0:T(8,128)(2,1)S(1)}, u32[]{:S(2)}, u32[]{:S(2)}) collective-permute-start(bf16[1,512,384]{2,1,0:T(8,128)(2,1)S(1)} %get-tuple-element.112), channel_id=1, source_target_pairs={{16,0},{17,1},{18,2},{19,3},{20,4},{21,5},{22,6},{23,7},{24,8},{25... | collective-permute-start | bytes 1179656 | tf_op jit(solution)/shard_map/ppermute | solution.py:740
  220.8 27.2 %slice-start.1 = ((s8[4718592]{0:T(1024)(128)(4,1)}), s8[524288]{0:T(1024)(128)(4,1)S(1)}, s32[]{:S(2)}) async-start(s8[4718592]{0:T(1024)(128)(4,1)} %bitcast.97), calls=%async_computation.4 | async-start | bytes 1048576
  220.8 15.7 %collective-permute-start.17 = (f32[2,2,3,2,512]{4,3,2,1,0:T(2,128)S(1)}, f32[2,2,3,2,512]{4,3,2,1,0:T(2,128)S(1)}, u32[]{:S(2)}, u32[]{:S(2)}) collective-permute-start(f32[2,2,3,2,512]{4,3,2,1,0:T(2,128)S(1)} %pad_maximum_fusion.9), channel_id=1, source_target_pairs={{16,0},{17,1},{18,2},{19,3},{20,4},{21,5},{22,6},{23,7},{24,8},{25... | collective-permute-start | bytes 147464 | tf_op jit(solution)/shard_map/ppermute | solution.py:742
  232.6 37.9 %collective-permute-start.21 = (bf16[1,512,384]{2,1,0:T(8,128)(2,1)}, bf16[1,512,384]{2,1,0:T(8,128)(2,1)}, u32[]{:S(2)}, u32[]{:S(2)}) collective-permute-start(bf16[1,512,384]{2,1,0:T(8,128)(2,1)} %get-tuple-element.111), channel_id=1, source_target_pairs={{16,0},{17,1},{18,2},{19,3},{20,4},{21,5},{22,6},{23,7},{24,8},{25... | collective-permute-start | bytes 1179656 | tf_op jit(solution)/shard_map/ppermute | solution.py:740
  244.4 47.7 %collective-permute-start.20 = (bf16[1,512,768]{2,1,0:T(8,128)(2,1)}, bf16[1,512,768]{2,1,0:T(8,128)(2,1)}, u32[]{:S(2)}, u32[]{:S(2)}) collective-permute-start(bf16[1,512,768]{2,1,0:T(8,128)(2,1)} %get-tuple-element.73.refs_0_.refs_6_.refs_9_), channel_id=1, source_target_pairs={{0,16},{16,0},{1,17},{17,1},{2,18},{18,2},{3,19},{19,3},{4,20},{20... | collective-permute-start | bytes 2359304 | tf_op jit(solution)/shard_map/ppermute | solution.py:778
  250.4 5.2 %copy-start.11 = (bf16[2,2,1,2,1,96,768]{6,5,4,3,2,1,0:T(8,128)(2,1)}, bf16[2,2,1,2,1,96,768]{6,5,4,3,2,1,0:T(8,128)(2,1)S(1)}, u32[]{:S(2)}) copy-start(bf16[2,2,1,2,1,96,768]{6,5,4,3,2,1,0:T(8,128)(2,1)S(1)} %constant_dynamic-slice_fusion.9.refs_1_) | copy-start | bytes 3538948
  250.4 38.7 %collective-permute-start.25 = (bf16[2,2,1,2,1,96,768]{6,5,4,3,2,1,0:T(8,128)(2,1)S(1)}, bf16[2,2,1,2,1,96,768]{6,5,4,3,2,1,0:T(8,128)(2,1)}, u32[]{:S(2)}, u32[]{:S(2)}) collective-permute-start(bf16[2,2,1,2,1,96,768]{6,5,4,3,2,1,0:T(8,128)(2,1)S(1)} %constant_dynamic-slice_fusion.9.refs_1_), channel_id=1, source_target_pairs={{0,4},{1,5},{2,6},{3,7},{4,0},{5,1},{6,2},{7,3},{8,12},{9,13},{10,... | collective-permute-start | bytes 3538952 | tf_op jit(solution)/shard_map/ppermute | solution.py:475
  258.5 50.4 %collective-permute-start.27 = (bf16[2,2,2,1,1,24,3840]{6,5,4,3,2,1,0:T(8,128)(2,1)}, bf16[2,2,2,1,1,24,3840]{6,5,4,3,2,1,0:T(8,128)(2,1)}, u32[]{:S(2)}, u32[]{:S(2)}) collective-permute-start(bf16[2,2,2,1,1,24,3840]{6,5,4,3,2,1,0:T(8,128)(2,1)} %constant_dynamic-slice_fusion.8.refs_2_), channel_id=1, source_target_pairs={{0,2},{1,3},{2,0},{3,1},{4,6},{5,7},{6,4},{7,5},{8,10},{9,11},{10,... | collective-permute-start | bytes 4423688 | tf_op jit(solution)/shard_map/ppermute | solution.py:475
  270.5 7.4 %copy-start.3 = (bf16[2,512,768]{2,1,0:T(8,128)(2,1)S(1)}, bf16[2,512,768]{2,1,0:T(8,128)(2,1)}, u32[]{:S(2)}) copy-start(bf16[2,512,768]{2,1,0:T(8,128)(2,1)} %param.15) | copy-start | bytes 4718596
  277.8 19.2 %collective-permute-start.22 = (bf16[1,512,768]{2,1,0:T(8,128)(2,1)}, bf16[1,512,768]{2,1,0:T(8,128)(2,1)}, u32[]{:S(2)}, u32[]{:S(2)}) collective-permute-start(bf16[1,512,768]{2,1,0:T(8,128)(2,1)} %get-tuple-element.78.refs_9_.refs_12_), channel_id=1, source_target_pairs={{0,16},{16,0},{1,17},{17,1},{2,18},{18,2},{3,19},{19,3},{4,20},{20... | collective-permute-start | bytes 2359304 | tf_op jit(solution)/shard_map/ppermute | solution.py:778
  290.7 6.4 %copy-start.13 = (bf16[2,2,1,2,1,96,768]{6,5,4,3,2,1,0:T(8,128)(2,1)}, bf16[2,2,1,2,1,96,768]{6,5,4,3,2,1,0:T(8,128)(2,1)S(1)}, u32[]{:S(2)}) copy-start(bf16[2,2,1,2,1,96,768]{6,5,4,3,2,1,0:T(8,128)(2,1)S(1)} %add_convert_fusion.5) | copy-start | bytes 3538948
  291.7 34.8 %collective-permute-start.26 = (bf16[2,2,1,1,1,96,768]{6,5,4,3,2,1,0:T(8,128)(2,1)}, bf16[2,2,1,1,1,96,768]{6,5,4,3,2,1,0:T(8,128)(2,1)}, u32[]{:S(2)}, u32[]{:S(2)}) collective-permute-start(bf16[2,2,1,1,1,96,768]{6,5,4,3,2,1,0:T(8,128)(2,1)} %constant_dynamic-slice_fusion.4), channel_id=1, source_target_pairs={{0,2},{1,3},{2,0},{3,1},{4,6},{5,7},{6,4},{7,5},{8,10},{9,11},{10,... | collective-permute-start | bytes 1769480 | tf_op jit(solution)/shard_map/ppermute | solution.py:475
  297.0 11.8 %copy-start.7 = (bf16[2,2,2,2,1,24,3840]{6,5,4,3,2,1,0:T(8,128)(2,1)S(1)}, bf16[2,2,2,2,1,24,3840]{6,5,4,3,2,1,0:T(8,128)(2,1)}, u32[]{:S(2)}) copy-start(bf16[2,2,2,2,1,24,3840]{6,5,4,3,2,1,0:T(8,128)(2,1)} %copy-done.6) | copy-start | bytes 8847364
  307.5 4.6 %collective-permute-start.23 = (bf16[2,2,2,2,1,24,1152]{6,5,4,3,2,1,0:T(8,128)(2,1)}, bf16[2,2,2,2,1,24,1152]{6,5,4,3,2,1,0:T(8,128)(2,1)}, u32[]{:S(2)}, u32[]{:S(2)}) collective-permute-start(bf16[2,2,2,2,1,24,1152]{6,5,4,3,2,1,0:T(8,128)(2,1)} %constant_dynamic-slice_fusion.7), channel_id=1, source_target_pairs={{0,1},{1,0},{2,3},{3,2},{4,5},{5,4},{6,7},{7,6},{8,9},{9,8},{10,11... | collective-permute-start | bytes 2654216 | tf_op jit(solution)/shard_map/ppermute | solution.py:475
  310.7 4.4 %copy-start.9 = (bf16[2,2,2,1,1,24,3840]{6,5,4,3,2,1,0:T(8,128)(2,1)}, bf16[2,2,2,1,1,24,3840]{6,5,4,3,2,1,0:T(8,128)(2,1)S(1)}, u32[]{:S(2)}) copy-start(bf16[2,2,2,1,1,24,3840]{6,5,4,3,2,1,0:T(8,128)(2,1)S(1)} %add_convert_fusion.4) | copy-start | bytes 4423684
  311.7 21.1 %collective-permute-start.28 = (bf16[1,2,2,1,1,24,3840]{6,5,4,3,2,1,0:T(8,128)(2,1)}, bf16[1,2,2,1,1,24,3840]{6,5,4,3,2,1,0:T(8,128)(2,1)}, u32[]{:S(2)}, u32[]{:S(2)}) collective-permute-start(bf16[1,2,2,1,1,24,3840]{6,5,4,3,2,1,0:T(8,128)(2,1)} %constant_dynamic-slice_fusion.3), channel_id=1, source_target_pairs={{0,16},{16,0},{1,17},{17,1},{2,18},{18,2},{3,19},{19,3},{4,20},{20... | collective-permute-start | bytes 2211848 | tf_op jit(solution)/shard_map/ppermute | solution.py:473
  315.2 36.0 %collective-permute-start.29 = (bf16[1,2,2,2,1,24,1152]{6,5,4,3,2,1,0:T(8,128)(2,1)}, bf16[1,2,2,2,1,24,1152]{6,5,4,3,2,1,0:T(8,128)(2,1)}, u32[]{:S(2)}, u32[]{:S(2)}) collective-permute-start(bf16[1,2,2,2,1,24,1152]{6,5,4,3,2,1,0:T(8,128)(2,1)} %constant_dynamic-slice_fusion.6.refs_0_), channel_id=1, source_target_pairs={{0,16},{16,0},{1,17},{17,1},{2,18},{18,2},{3,19},{19,3},{4,20},{20... | collective-permute-start | bytes 1327112 | tf_op jit(solution)/shard_map/ppermute | solution.py:473
  326.3 11.0 %collective-permute-start.24 = (bf16[2,2,2,2,1,24,1152]{6,5,4,3,2,1,0:T(8,128)(2,1)S(1)}, bf16[2,2,2,2,1,24,1152]{6,5,4,3,2,1,0:T(8,128)(2,1)}, u32[]{:S(2)}, u32[]{:S(2)}) collective-permute-start(bf16[2,2,2,2,1,24,1152]{6,5,4,3,2,1,0:T(8,128)(2,1)S(1)} %constant_dynamic-slice_fusion.5.refs_1_), channel_id=1, source_target_pairs={{0,1},{1,0},{2,3},{3,2},{4,5},{5,4},{6,7},{7,6},{8,9},{9,8},{10,11... | collective-permute-start | bytes 2654216 | tf_op jit(solution)/shard_map/ppermute | solution.py:475
  327.3 5.5 %copy-start.10 = (bf16[2,2,2,1,1,24,3840]{6,5,4,3,2,1,0:T(8,128)(2,1)S(1)}, bf16[2,2,2,1,1,24,3840]{6,5,4,3,2,1,0:T(8,128)(2,1)}, u32[]{:S(2)}) copy-start(bf16[2,2,2,1,1,24,3840]{6,5,4,3,2,1,0:T(8,128)(2,1)} %copy-done.9) | copy-start | bytes 4423684
  330.4 37.6 %collective-permute-start.31 = (bf16[2,1,1,1,1,96,768]{6,5,4,3,2,1,0:T(8,128)(2,1)}, bf16[2,1,1,1,1,96,768]{6,5,4,3,2,1,0:T(8,128)(2,1)}, u32[]{:S(2)}, u32[]{:S(2)}) collective-permute-start(bf16[2,1,1,1,1,96,768]{6,5,4,3,2,1,0:T(8,128)(2,1)} %dynamic-slice_convert_fusion.1.refs_1_), channel_id=1, source_target_pairs={{0,8},{1,9},{2,10},{3,11},{4,12},{5,13},{6,14},{7,15},{8,0},{9,1},... | collective-permute-start | bytes 884744 | tf_op jit(solution)/shard_map/ppermute | solution.py:475
  336.0 35.2 %collective-permute-start.33 = (bf16[1,2,1,1,1,24,3840]{6,5,4,3,2,1,0:T(8,128)(2,1)}, bf16[1,2,1,1,1,24,3840]{6,5,4,3,2,1,0:T(8,128)(2,1)}, u32[]{:S(2)}, u32[]{:S(2)}) collective-permute-start(bf16[1,2,1,1,1,24,3840]{6,5,4,3,2,1,0:T(8,128)(2,1)} %dynamic-slice_convert_fusion.refs_2_), channel_id=1, source_target_pairs={{0,4},{1,5},{2,6},{3,7},{4,0},{5,1},{6,2},{7,3},{8,12},{9,13},{10,... | collective-permute-start | bytes 1105928 | tf_op jit(solution)/shard_map/ppermute | solution.py:475
  339.6 25.9 %collective-permute-start.32 = (bf16[2,2,2,1,1,24,1152]{6,5,4,3,2,1,0:T(8,128)(2,1)}, bf16[2,2,2,1,1,24,1152]{6,5,4,3,2,1,0:T(8,128)(2,1)}, u32[]{:S(2)}, u32[]{:S(2)}) collective-permute-start(bf16[2,2,2,1,1,24,1152]{6,5,4,3,2,1,0:T(8,128)(2,1)} %constant_dynamic-slice_fusion.2.refs_0_), channel_id=1, source_target_pairs={{0,2},{1,3},{2,0},{3,1},{4,6},{5,7},{6,4},{7,5},{8,10},{9,11},{10,... | collective-permute-start | bytes 1327112 | tf_op jit(solution)/shard_map/ppermute | solution.py:475
  340.1 11.1 %copy-start.20 = (bf16[2,2,2,2,1,24,1152]{6,5,4,3,2,1,0:T(8,128)(2,1)S(1)}, bf16[2,2,2,2,1,24,1152]{6,5,4,3,2,1,0:T(8,128)(2,1)}, u32[]{:S(2)}) copy-start(bf16[2,2,2,2,1,24,1152]{6,5,4,3,2,1,0:T(8,128)(2,1)} %copy-done.19) | copy-start | bytes 2654212
  340.1 12.5 %copy-start.37 = (f32[32,24]{1,0:T(8,128)S(1)}, f32[32,24]{1,0:T(8,128)}, u32[]{:S(2)}) copy-start(f32[32,24]{1,0:T(8,128)} %reshape_squeeze.21) | copy-start | bytes 9220
  340.1 12.5 %copy-start.38 = (f32[32,24]{1,0:T(8,128)S(1)}, f32[32,24]{1,0:T(8,128)}, u32[]{:S(2)}) copy-start(f32[32,24]{1,0:T(8,128)} %reshape_squeeze.22) | copy-start | bytes 9220
  340.1 12.5 %copy-start.39 = (f32[32,24]{1,0:T(8,128)S(1)}, f32[32,24]{1,0:T(8,128)}, u32[]{:S(2)}) copy-start(f32[32,24]{1,0:T(8,128)} %reshape_squeeze.23) | copy-start | bytes 9220
  340.1 12.5 %copy-start.40 = (f32[32,96]{1,0:T(8,128)S(1)}, f32[32,96]{1,0:T(8,128)}, u32[]{:S(2)}) copy-start(f32[32,96]{1,0:T(8,128)} %reshape.202) | copy-start | bytes 36868
  340.1 12.5 %copy-start.41 = (f32[32,24]{1,0:T(8,128)S(1)}, f32[32,24]{1,0:T(8,128)}, u32[]{:S(2)}) copy-start(f32[32,24]{1,0:T(8,128)} %reshape.200) | copy-start | bytes 9220
  340.1 12.5 %copy-start.42 = (f32[32,24]{1,0:T(8,128)S(1)}, f32[32,24]{1,0:T(8,128)}, u32[]{:S(2)}) copy-start(f32[32,24]{1,0:T(8,128)} %reshape.201) | copy-start | bytes 9220
  352.3 13.1 %copy-start.22 = (bf16[1,2,2,2,1,24,1152]{6,5,4,3,2,1,0:T(8,128)(2,1)}, bf16[1,2,2,2,1,24,1152]{6,5,4,3,2,1,0:T(8,128)(2,1)S(1)}, u32[]{:S(2)}) copy-start(bf16[1,2,2,2,1,24,1152]{6,5,4,3,2,1,0:T(8,128)(2,1)S(1)} %add_convert_fusion.9) | copy-start | bytes 1327108
  352.3 15.7 %copy-start.18 = (f32[2,2,1,1,1,96,768]{6,5,4,3,2,1,0:T(8,128)S(1)}, f32[2,2,1,1,1,96,768]{6,5,4,3,2,1,0:T(8,128)}, u32[]{:S(2)}) copy-start(f32[2,2,1,1,1,96,768]{6,5,4,3,2,1,0:T(8,128)} %copy-done.17) | copy-start | bytes 3538948
  353.4 10.8 %all-to-all-start = ((f32[32,1,288]{2,1,0:T(1,128)}), f32[32,1,288]{2,1,0:T(1,128)S(1)}, u32[]{:S(2)}, u32[]{:S(2)}) async-start(f32[32,1,288]{2,1,0:T(1,128)} %all_to_all.6), calls=%async_computation | async-start | bytes 98304 | tf_op jit(solution)/shard_map/all_to_all | solution.py:812
  357.5 15.5 %collective-permute-start.30 = (bf16[1,2,2,1,1,24,1152]{6,5,4,3,2,1,0:T(8,128)(2,1)}, bf16[1,2,2,1,1,24,1152]{6,5,4,3,2,1,0:T(8,128)(2,1)}, u32[]{:S(2)}, u32[]{:S(2)}) collective-permute-start(bf16[1,2,2,1,1,24,1152]{6,5,4,3,2,1,0:T(8,128)(2,1)} %constant_dynamic-slice_fusion.1.refs_1_), channel_id=1, source_target_pairs={{0,2},{1,3},{2,0},{3,1},{4,6},{5,7},{6,4},{7,5},{8,10},{9,11},{10,... | collective-permute-start | bytes 663560 | tf_op jit(solution)/shard_map/ppermute | solution.py:475
  367.4 8.5 %collective-permute-start.34 = (bf16[1,2,2,1,1,24,1152]{6,5,4,3,2,1,0:T(8,128)(2,1)S(1)}, bf16[1,2,2,1,1,24,1152]{6,5,4,3,2,1,0:T(8,128)(2,1)}, u32[]{:S(2)}, u32[]{:S(2)}) collective-permute-start(bf16[1,2,2,1,1,24,1152]{6,5,4,3,2,1,0:T(8,128)(2,1)S(1)} %constant_dynamic-slice_fusion.refs_2_), channel_id=1, source_target_pairs={{0,16},{16,0},{1,17},{17,1},{2,18},{18,2},{3,19},{19,3},{4,20},{20... | collective-permute-start | bytes 663560 | tf_op jit(solution)/shard_map/ppermute | solution.py:473
  369.8 8.3 %collective-permute-start.38 = (bf16[1,1,1,1,1,96,768]{6,5,4,3,2,1,0:T(8,128)(2,1)}, bf16[1,1,1,1,1,96,768]{6,5,4,3,2,1,0:T(8,128)(2,1)}, u32[]{:S(2)}, u32[]{:S(2)}) collective-permute-start(bf16[1,1,1,1,1,96,768]{6,5,4,3,2,1,0:T(8,128)(2,1)} %dynamic-slice_convert_fusion.3.refs_1_), channel_id=1, source_target_pairs={{0,16},{16,0},{1,17},{17,1},{2,18},{18,2},{3,19},{19,3},{4,20},{20... | collective-permute-start | bytes 442376 | tf_op jit(solution)/shard_map/ppermute | solution.py:473
  372.4 14.2 %collective-permute-start.37 = (bf16[1,1,1,1,1,24,3840]{6,5,4,3,2,1,0:T(8,128)(2,1)S(1)}, bf16[1,1,1,1,1,24,3840]{6,5,4,3,2,1,0:T(8,128)(2,1)S(1)}, u32[]{:S(2)}, u32[]{:S(2)}) collective-permute-start(bf16[1,1,1,1,1,24,3840]{6,5,4,3,2,1,0:T(8,128)(2,1)S(1)} %dynamic-slice_convert_fusion.2.refs_2_), channel_id=1, source_target_pairs={{0,8},{1,9},{2,10},{3,11},{4,12},{5,13},{6,14},{7,15},{8,0},{9,1},... | collective-permute-start | bytes 552968 | tf_op jit(solution)/shard_map/ppermute | solution.py:475
  376.9 9.5 %collective-permute-start.35 = (bf16[1,2,1,1,1,24,2304]{6,5,4,3,2,1,0:T(8,128)(2,1)S(1)}, bf16[1,2,1,1,1,24,2304]{6,5,4,3,2,1,0:T(8,128)(2,1)S(1)}, u32[]{:S(2)}, u32[]{:S(2)}) collective-permute-start(bf16[1,2,1,1,1,24,2304]{6,5,4,3,2,1,0:T(8,128)(2,1)S(1)} %fusion.5), channel_id=1, source_target_pairs={{0,4},{1,5},{2,6},{3,7},{4,0},{5,1},{6,2},{7,3},{8,12},{9,13},{10,... | collective-permute-start | bytes 663560 | tf_op jit(solution)/shard_map/ppermute | solution.py:475
  386.4 5.9 %collective-permute-start.36 = (bf16[1,1,1,1,1,24,2304]{6,5,4,3,2,1,0:T(8,128)(2,1)S(1)}, bf16[1,1,1,1,1,24,2304]{6,5,4,3,2,1,0:T(8,128)(2,1)S(1)}, u32[]{:S(2)}, u32[]{:S(2)}) collective-permute-start(bf16[1,1,1,1,1,24,2304]{6,5,4,3,2,1,0:T(8,128)(2,1)S(1)} %dynamic-slice_convert_fusion.4), channel_id=1, source_target_pairs={{0,8},{1,9},{2,10},{3,11},{4,12},{5,13},{6,14},{7,15},{8,0},{9,1},... | collective-permute-start | bytes 331784 | tf_op jit(solution)/shard_map/ppermute | solution.py:475
  (27 other events, 44.7 us)
Sparse Core Ops, SparseCore 0:
  10.9 69.2 all-gather.4
  83.7 71.4 all-gather.2
